TPU v7x, 32 devices: a whole 2x2x4 slice. The times are simulated.
32 devices in a mesh: grp: 4 (over y, core), cls: 8 (over z, x).
Axes of the slice: x: 2, y: 2, z: 4, core: 2. Of those that a mesh axis runs over, the one named last changes fastest.
Arguments:
- particles: float32 [1024, 128, 128], P(('grp', 'cls')), may hold values from -6 to 6
- references: float32 [256, 2, 128, 128], P('cls'), may hold values from -6 to 6
- class_of: int32 [1024], P(('grp', 'cls')), may hold values from 0 to 255, as said below
- rotation_bin: int32 [1024], P(('grp', 'cls')), may hold values from 0 to 3
- shift_best: int32 [1024], P(('grp', 'cls')), may hold values from 0 to 63
- defocus_bin: int32 [1024], P(('grp', 'cls')), may hold values from 0 to 15
- shift_list: int32 [64, 2], replicated, may hold values from -8 to 8
- defocus: float32 [16], replicated, may hold values from 8 to 64
Outputs:
- scores: float32 [1024, 64], P(('grp', 'cls'))
- new_references: float32 [256, 2, 128, 128], P(('cls', 'grp'))
Inputs may be any that keep to these rules, and one draw needn't show every extreme that they name: `class_of`: class c belongs to owner c // 32. Among the 32 particles of one device (aligned blocks of 32 rows), at most 8 belong to the classes of one owner, and in every draw one owner holds exactly 8 from every device.
All inputs are finite; a program needn't handle non-finite values.
Results may differ from a plain program's by a relative error of at most 0.0003.
Values sent between devices are 32-bit elements; how exact they have to be, the bound alone decides.
A program may use at most 128 MiB of HBM per device.

v0:
```python
import functools
import math

import jax
import jax.numpy as jnp
from jax import lax
from jax.experimental import pallas as pl
from jax.experimental.pallas import tpu as pltpu
from jax.sharding import PartitionSpec as P

f32, bf16 = jnp.float32, jnp.bfloat16
HALF = 72
GROUP = 8
VMEM_BYTES = 56 * 1024 * 1024


def split(x):
    high = x.astype(bf16)
    return high, (x - high.astype(f32)).astype(bf16)


def split_table(x):
    high = lax.reduce_precision(x, 8, 7)
    return high.astype(bf16), lax.reduce_precision(x - high, 8, 7).astype(bf16)


def dot(a, b):
    return jnp.dot(a, b, preferred_element_type=f32)


def dot3(a, b):
    return dot(a[0], b[0]) + (dot(a[1], b[0]) + dot(a[0], b[1]))


def circle(turns, side):
    angles = (turns % side).astype(f32) * (2.0 * math.pi / side)
    return jnp.cos(angles), jnp.sin(angles)


def dft_tables(side):
    pixel = jnp.arange(side, dtype=jnp.int32)
    norm = 1.0 / math.sqrt(side)
    cos_table, sin_table = circle(pixel[:, None] * pixel[None, :], side)
    cos_table, sin_table = cos_table * norm, sin_table * norm
    flip_cos, flip_sin = circle(pixel[:, None] * (side - 1 - pixel)[None, :], side)
    flip_cos, flip_sin = flip_cos * norm, flip_sin * norm
    right = jnp.stack(
        [
            jnp.concatenate([cos_table, sin_table], axis=1),
            jnp.concatenate([flip_cos.T, flip_sin.T], axis=1),
        ]
    )
    live = (jnp.arange(HALF) <= side // 2)[:, None].astype(f32)

    def left(c, s):
        c, s = c[:HALF] * live, s[:HALF] * live
        return jnp.concatenate(
            [jnp.concatenate([c, -s], axis=1), jnp.concatenate([-s, -c], axis=1)], axis=0
        )

    return right, jnp.stack([left(cos_table, sin_table), left(flip_cos, flip_sin)])


def contrast_half(defocus, side):
    pixel = jnp.arange(side, dtype=jnp.int32)
    signed = jnp.where(pixel < side // 2, pixel, pixel - side).astype(f32)
    rows = signed[:HALF]
    radius = (rows[:, None] * rows[:, None] + signed[None, :] * signed[None, :]) / float(
        (side // 2) ** 2
    )
    phases = defocus[:, None, None] * radius[None]
    return -(0.995 * jnp.sin(phases) + 0.1 * jnp.cos(phases))


def shift_tables(shift_list, side):
    row_cos, row_sin = circle(
        shift_list[:, 0][:, None] * jnp.arange(HALF, dtype=jnp.int32)[None, :], side
    )
    col_cos, col_sin = circle(
        shift_list[:, 1][:, None] * jnp.arange(side, dtype=jnp.int32)[None, :], side
    )
    rc, rs = row_cos[:, :, None], row_sin[:, :, None]
    cc, cs = col_cos[:, None, :], col_sin[:, None, :]
    phase = jnp.stack([rc * cc - rs * cs, rs * cc + rc * cs], axis=1)
    score_right = jnp.concatenate([col_cos.T, col_sin.T], axis=1)
    row = jnp.arange(HALF)
    times = jnp.where(
        (row == 0) | (row == side // 2), 1.0, jnp.where(row < side // 2, 2.0, 0.0)
    ).astype(f32)[:, None] / side
    uc, us = row_cos.T * times, row_sin.T * times
    score_left = jnp.concatenate(
        [jnp.concatenate([uc, -us], axis=1), jnp.concatenate([-us, -uc], axis=1)], axis=0
    )
    return phase, score_right, score_left


def mirror_pick(rows, cols, side, offset):
    i = lax.broadcasted_iota(jnp.int32, (rows, cols), 0)
    j = lax.broadcasted_iota(jnp.int32, (rows, cols), 1)
    return jnp.where((i + j) % side == offset, 1.0, 0.0).astype(bf16)


def mirrored(x, row_pick, col_pick):
    total = None
    for piece in split(x):
        turned = dot(dot(row_pick, piece).astype(bf16), col_pick)
        total = turned if total is None else total + turned
    return total


def reference_half_kernel(side, ref, out):
    row_pick = mirror_pick(HALF, side, side, 0)
    col_pick = mirror_pick(side, side, side, 0)
    live = lax.broadcasted_iota(jnp.int32, (HALF, side), 0) <= side // 2
    for n in range(ref.shape[0]):
        for part, sign in ((0, 1.0), (1, -1.0)):
            x = ref[n, part]
            both = 0.5 * (x[:HALF] + sign * mirrored(x, row_pick, col_pick))
            out[n, part] = jnp.where(live, both, 0.0)


def reference_half(references):
    count, _, side, _ = references.shape
    step = math.gcd(count, 4)
    return pl.pallas_call(
        functools.partial(reference_half_kernel, side),
        grid=(count // step,),
        in_specs=[pl.BlockSpec((step, 2, side, side), lambda i: (i, 0, 0, 0))],
        out_specs=pl.BlockSpec((step, 2, HALF, side), lambda i: (i, 0, 0, 0)),
        out_shape=jax.ShapeDtypeStruct((count, 2, HALF, side), f32),
        compiler_params=pltpu.CompilerParams(vmem_limit_bytes=VMEM_BYTES),
        cost_estimate=pl.CostEstimate(
            flops=count * 2 * 8 * HALF * side * side, bytes_accessed=count * 4 * 200 * side * 2,
            transcendentals=0,
        ),
        name="reference_half",
    )(references)


def owner_kernel(
    side, info, images, refs, contrast, phase, right_hi, right_lo, left_hi, left_lo,
    sr_hi, sr_lo, score_left, start, scores, total,
):
    @pl.when(pl.program_id(0) == 0)
    def _():
        total[...] = start[...]

    base = pl.program_id(0) * GROUP
    lane = lax.broadcasted_iota(jnp.int32, (8, side), 1)
    tail_row = lax.broadcasted_iota(jnp.int32, (8, side), 0)
    rows = []
    for n in range(GROUP):
        local, bin_at, shift = info[0, base + n], info[1, base + n], info[2, base + n]
        turns, live = info[3, base + n], info[4, base + n].astype(f32)
        image = images[n]
        image = jnp.where(turns % 2 == 1, image.T, image)
        right_at = (turns >= 2).astype(jnp.int32)
        left_at = ((turns == 1) | (turns == 2)).astype(jnp.int32)
        halfway = dot3(split(image), (right_hi[right_at], right_lo[right_at]))
        halfway = jnp.concatenate([halfway[:, :side], halfway[:, side:]], axis=0)
        spec = dot3((left_hi[left_at], left_lo[left_at]), split(halfway))
        gain = contrast[bin_at] * live
        re, im = spec[:HALF] * gain, spec[HALF:] * gain
        ref_re, ref_im = refs[local, 0], refs[local, 1]
        product = jnp.concatenate([re * ref_re + im * ref_im, im * ref_re - re * ref_im], axis=0)
        part = dot3(split(product), (sr_hi[...], sr_lo[...]))
        rows.append(jnp.sum(part * score_left[...], axis=0, keepdims=True))
        cos, sin = phase[shift, 0], phase[shift, 1]
        con_re, con_im = re * cos - im * sin, im * cos + re * sin
        tail = jnp.where((tail_row == 1) & (lane == bin_at), live, con_re[side // 2 :])
        total[local, : side // 2] += con_re[: side // 2]
        total[local, side // 2 : HALF] += tail
        total[local, HALF:] += con_im
    found = jnp.concatenate(rows, axis=0)
    scores[...] = found + pltpu.roll(found, found.shape[1] // 2, 1)


def owner_terms(images, info, start, refs, tables):
    count, side, _ = images.shape
    contrast, phase, right, left, score_right, score_left = tables
    whole = lambda x: pl.BlockSpec(
        x.shape, lambda i, info: (0,) * x.ndim, pipeline_mode=pl.Buffered(1)
    )
    fixed = (refs, contrast, phase, *right, *left, *score_right, score_left, start)
    lanes = score_left.shape[1]
    return pl.pallas_call(
        functools.partial(owner_kernel, side),
        grid_spec=pltpu.PrefetchScalarGridSpec(
            num_scalar_prefetch=1,
            grid=(count // GROUP,),
            in_specs=[pl.BlockSpec((GROUP, side, side), lambda i, info: (i, 0, 0))]
            + [whole(x) for x in fixed],
            out_specs=[
                pl.BlockSpec((GROUP, lanes), lambda i, info: (i, 0)),
                pl.BlockSpec(start.shape, lambda i, info: (0, 0, 0)),
            ],
        ),
        out_shape=[
            jax.ShapeDtypeStruct((count, lanes), f32),
            jax.ShapeDtypeStruct(start.shape, f32),
        ],
        compiler_params=pltpu.CompilerParams(vmem_limit_bytes=VMEM_BYTES),
        cost_estimate=pl.CostEstimate(
            flops=count * 70_000_000, bytes_accessed=count * side * side * 4 + 14_000_000,
            transcendentals=0,
        ),
        name="owner_terms",
    )(info, images, *fixed)


def finish_kernel(side, bins, share, contrast, out):
    row_pick = mirror_pick(side // 2, HALF, side, side // 2)
    col_pick = mirror_pick(side, side, side, 0)
    tail_row = lax.broadcasted_iota(jnp.int32, (8, side), 0)
    middle = side // 2
    for n in range(share.shape[0]):
        counts = share[n, middle + 1 : middle + 2]
        weight = jnp.ones((HALF, side), f32)
        for d in range(bins):
            weight += counts[:, d : d + 1] * (contrast[d] * contrast[d])
        live = lax.broadcasted_iota(jnp.int32, (HALF, side), 0) <= middle
        for part, sign in ((0, 1.0), (1, -1.0)):
            fresh = jnp.where(live, share[n, part * HALF : (part + 1) * HALF], 0.0) / weight
            other = sign * mirrored(fresh, row_pick, col_pick)
            out[n, part, :middle] = fresh[:middle]
            out[n, part, middle : middle + 8] = jnp.where(tail_row == 0, fresh[middle:], other[:8])
            out[n, part, middle + 8 :] = other[8:]


def finish(share, contrast):
    count, _, side = share.shape
    return pl.pallas_call(
        functools.partial(finish_kernel, side, contrast.shape[0]),
        out_shape=jax.ShapeDtypeStruct((count, 2, side, side), f32),
        compiler_params=pltpu.CompilerParams(vmem_limit_bytes=VMEM_BYTES),
        cost_estimate=pl.CostEstimate(
            flops=count * 20_000_000, bytes_accessed=4_000_000, transcendentals=0
        ),
        name="finish",
    )(share, contrast)


def body(
    particles, references, class_of, rotation_bin, shift_best, defocus_bin, shift_list, defocus
):
    side = particles.shape[-1]
    part_rows = particles.shape[0]
    class_local = references.shape[0]
    shifts = shift_list.shape[0]
    owners = lax.axis_size("cls")
    capacity = max(2, 2 * part_rows // owners)
    chunk = capacity // 2
    slot_total = owners * capacity

    owner_of = class_of // class_local
    before = jnp.arange(part_rows)[:, None] > jnp.arange(part_rows)[None, :]
    rank = jnp.sum((before & (owner_of[:, None] == owner_of[None, :])).astype(jnp.int32), axis=1)
    target = (rank // chunk) * (owners * chunk) + owner_of * chunk + rank % chunk
    hit = target[None, :] == jnp.arange(slot_total, dtype=jnp.int32)[:, None]
    values = jnp.stack(
        [class_of % class_local, defocus_bin, shift_best, rotation_bin, jnp.ones_like(class_of)]
    )
    info = jnp.sum(jnp.where(hit[None], values[:, None, :], 0), axis=2).astype(f32)
    source = jnp.sum(
        jnp.where(hit, jnp.arange(part_rows, dtype=jnp.int32)[None, :], 0), axis=1
    ).reshape(2, owners * chunk)
    send = [particles[source[h]].reshape(owners, chunk, side, side) for h in (0, 1)]

    exchange = lambda x: lax.all_to_all(x, "cls", split_axis=0, concat_axis=0, tiled=True)
    info = info.reshape(5, 2, owners, chunk).transpose(2, 1, 0, 3)
    got = [exchange(send[0])]
    info = exchange(info).astype(jnp.int32).transpose(1, 2, 0, 3).reshape(2, 5, owners * chunk)
    got.append(exchange(send[1]))

    right, left = dft_tables(side)
    contrast = contrast_half(defocus, side)
    phase, score_right, score_left = shift_tables(shift_list, side)
    tables = (contrast, phase, split_table(right), split_table(left), split_table(score_right), score_left)
    refs = reference_half(references)

    total = jnp.zeros((class_local, 2 * HALF, side), f32)
    found = []
    for h in (0, 1):
        scores, total = owner_terms(
            got[h].reshape(owners * chunk, side, side), info[h], total, refs, tables
        )
        found.append(scores[:, :shifts].reshape(owners, chunk, shifts))
    share = lax.psum_scatter(total, "grp", scatter_dimension=0, tiled=True)
    home = exchange(jnp.concatenate(found, axis=1))
    home = home.reshape(owners, 2, chunk, shifts).transpose(1, 0, 2, 3)
    scores = home.reshape(slot_total, shifts)[target]
    return scores, finish(share, contrast)


def solution(mesh):
    return jax.shard_map(
        body,
        mesh=mesh,
        in_specs=(
            P(("grp", "cls"), None, None),
            P("cls", None, None, None),
            P(("grp", "cls")),
            P(("grp", "cls")),
            P(("grp", "cls")),
            P(("grp", "cls")),
            P(),
            P(),
        ),
        out_specs=(P(("grp", "cls"), None), P(("cls", "grp"), None, None, None)),
        check_vma=False,
    )
```

profile of v0, /device:TPU:0, one launch (start us, length us, event | category | flops | bytes accessed | tf_op | source)
XLA Modules:
  0.0 188.5 jit_solution(14925278621877132208)
XLA Ops:
  7.2 0.8 and_select_fusion.3
  8.3 0.7 stack.42
  9.2 0.8 copy.16
  10.0 7.3 %all-to-all-start = ((f32[8,2,5,4]{2,3,1,0:T(4,128)}), f32[8,2,5,4]{2,3,1,0:T(4,128)S(1)}, u32[]{:S(2)}, u32[]{:S(2)}) async-start(f32[8,2,5,4]{2,3,1,0:T(4,128)} %copy.16), calls=%async_computation | async-start | bytes 65536 | tf_op jit(solution)/shard_map/all_to_all | solution.py:269
  17.4 2.0 %gather_fusion = f32[32,128,128]{2,1,0:T(8,128)} fusion(f32[32,128,128]{2,1,0:T(8,128)S(1)} %copy-done, s32[1024]{0:T(1024)S(1)} %get-tuple-element.51), kind=kCustom, calls=%fused_computation | custom fusion | bytes 4194432 | tf_op jit(solution)/shard_map/gather | solution.py:267
  19.4 4.5 %all-to-all-done = f32[8,2,5,4]{2,3,1,0:T(4,128)S(1)} async-done(((f32[8,2,5,4]{2,3,1,0:T(4,128)}), f32[8,2,5,4]{2,3,1,0:T(4,128)S(1)}, u32[]{:S(2)}, u32[]{:S(2)}) %all-to-all-start) | async-done | bytes 1312 | tf_op jit(solution)/shard_map/all_to_all | solution.py:269
  23.9 4.3 %all-to-all-start.1 = ((f32[8,4,128,128]{3,2,1,0:T(8,128)}), f32[8,4,128,128]{3,2,1,0:T(8,128)}, u32[]{:S(2)}, u32[]{:S(2)}) async-start(f32[8,4,128,128]{3,2,1,0:T(8,128)} %bitcast.35), calls=%async_computation.1 | async-start | bytes 4194304 | tf_op jit(solution)/shard_map/all_to_all | solution.py:269
  28.3 2.0 %gather_fusion.1 = f32[32,128,128]{2,1,0:T(8,128)} fusion(f32[32,128,128]{2,1,0:T(8,128)S(1)} %copy-done, s32[1024]{0:T(1024)S(1)} %get-tuple-element.50), kind=kCustom, calls=%fused_computation.1 | custom fusion | bytes 4194432 | tf_op jit(solution)/shard_map/gather | solution.py:267
  30.6 0.7 fusion.9
  31.5 0.7 maximum_maximum_fusion.score_left
  32.3 43.1 %all-to-all-done.1 = f32[8,4,128,128]{3,2,1,0:T(8,128)} async-done(((f32[8,4,128,128]{3,2,1,0:T(8,128)}), f32[8,4,128,128]{3,2,1,0:T(8,128)}, u32[]{:S(2)}, u32[]{:S(2)}) %all-to-all-start.1) | async-done | bytes 2097184 | tf_op jit(solution)/shard_map/all_to_all | solution.py:269
  75.4 4.3 %all-to-all-start.2 = ((f32[8,4,128,128]{3,2,1,0:T(8,128)}), f32[8,4,128,128]{3,2,1,0:T(8,128)}, u32[]{:S(2)}, u32[]{:S(2)}) async-start(f32[8,4,128,128]{3,2,1,0:T(8,128)} %bitcast.34), calls=%async_computation.2 | async-start | bytes 4194304 | tf_op jit(solution)/shard_map/all_to_all | solution.py:269
  79.8 10.1 %reference_half.1.refs = f32[32,2,72,128]{3,2,1,0:T(8,128)} custom-call(f32[32,2,128,128]{3,2,1,0:T(8,128)} %ref.1), custom_call_target="tpu_custom_call" | custom-call | flops 603979776 | bytes 6553600 | tf_op jit(solution)/shard_map/reference_half/pallas_call | solution.py:125
  90.7 0.8 fusion.7
  91.5 0.7 fusion.5
  92.8 1.3 multiply_subtract_fusion
  94.0 2.4 %pad_maximum_fusion.phase = f32[64,2,72,128]{3,2,1,0:T(8,128)} fusion(f32[64,1,72,128]{3,2,1,0:T(8,128)S(1)} %get-tuple-element.23, f32[64,1,72,128]{3,2,1,0:T(8,128)S(1)} %get-tuple-element.22), kind=kLoop, calls=%fused_computation.3 | loop fusion | flops 1179648 | bytes 9437184 | tf_op jit(solution)/shard_map/stack | solution.py:84
  96.5 3.2 %fusion.2.contrast = f32[16,72,128]{2,1,0:T(8,128)} fusion(f32[72,128]{1,0:T(8,128)S(1)} %add_multiply_fusion, f32[16]{0:T(128)S(1)} %copy-done.4), kind=kLoop, calls=%fused_computation.10 | loop fusion | flops 737280 | bytes 626752 | tf_op jit(solution)/shard_map/neg | solution.py:72
  99.7 0.7 copy.20.info
  100.3 0.7 copy.21.info
  101.0 1.6 broadcast_in_dim.92.start
  102.5 18.0 %owner_terms.2 = (f32[32,128]{1,0:T(8,128)}, f32[32,144,128]{2,1,0:T(8,128)}) custom-call(s32[5,32]{1,0:T(8,128)} %copy.20.info, f32[32,128,128]{2,1,0:T(8,128)} %bitcast.8.images, f32[32,2,72,128]{3,2,1,0:T(8,128)} %reference_half.1.refs, f32[16,72,128]{2,1,0:T(8,128)} %fusion.2.contrast, f32[64,2,72,128]{3,2,1,0:T(8,128)} %pad_maximum_fusion.phase, ...), custom_call_target="tpu_custom_call" | custom-call | flops 2240000000 | bytes 16097152 | tf_op jit(solution)/shard_map/owner_terms/pallas_call | solution.py:186
  120.6 6.9 %all-to-all-done.2 = f32[8,4,128,128]{3,2,1,0:T(8,128)} async-done(((f32[8,4,128,128]{3,2,1,0:T(8,128)}), f32[8,4,128,128]{3,2,1,0:T(8,128)}, u32[]{:S(2)}, u32[]{:S(2)}) %all-to-all-start.2) | async-done | bytes 2097184 | tf_op jit(solution)/shard_map/all_to_all | solution.py:269
  127.5 18.0 %owner_terms.3 = (f32[32,128]{1,0:T(8,128)}, f32[32,144,128]{2,1,0:T(8,128)}) custom-call(s32[5,32]{1,0:T(8,128)} %copy.21.info, f32[32,128,128]{2,1,0:T(8,128)} %bitcast.18.images, f32[32,2,72,128]{3,2,1,0:T(8,128)} %reference_half.1.refs, f32[16,72,128]{2,1,0:T(8,128)} %fusion.2.contrast, f32[64,2,72,128]{3,2,1,0:T(8,128)} %pad_maximum_fusion.phase, ...), custom_call_target="tpu_custom_call" | custom-call | flops 2240000000 | bytes 16097152 | tf_op jit(solution)/shard_map/owner_terms/pallas_call | solution.py:186
  145.5 0.7 copy-done.1
  146.2 0.7 reshape.287
  146.9 3.6 %all-to-all-start.3 = ((f32[8,1,512]{2,1,0:T(1,128)}), f32[8,1,512]{2,1,0:T(1,128)S(1)}, u32[]{:S(2)}, u32[]{:S(2)}) async-start(f32[8,1,512]{2,1,0:T(1,128)} %reshape.287), calls=%async_computation.3 | async-start | bytes 32768 | tf_op jit(solution)/shard_map/all_to_all | solution.py:269
  150.5 6.6 %all-to-all-done.3 = f32[8,1,512]{2,1,0:T(1,128)S(1)} async-done(((f32[8,1,512]{2,1,0:T(1,128)}), f32[8,1,512]{2,1,0:T(1,128)S(1)}, u32[]{:S(2)}, u32[]{:S(2)}) %all-to-all-start.3) | async-done | bytes 16416 | tf_op jit(solution)/shard_map/all_to_all | solution.py:269
  157.6 0.7 reduce
  158.3 1.2 gather_fusion.2
  159.5 18.2 %reduce-scatter.2.cloned.1.call-done.share = f32[8,144,128]{2,1,0:T(8,128)} async-done(((f32[32,144,128]{2,1,0:T(8,128)}), f32[8,144,128]{2,1,0:T(8,128)}) %reduce-scatter.2.cloned.1.call-update) | async-done | bytes 589840 | tf_op jit(solution)/shard_map/reduce_scatter | solution.py:288
  177.7 4.0 %finish.1 = f32[8,2,128,128]{3,2,1,0:T(8,128)} custom-call(f32[8,144,128]{2,1,0:T(8,128)} %reduce-scatter.2.cloned.1.call-done.share, f32[16,72,128]{2,1,0:T(8,128)} %fusion.2.contrast), custom_call_target="tpu_custom_call" | custom-call | flops 160000000 | bytes 4000000 | tf_op jit(solution)/shard_map/finish/pallas_call | solution.py:232
  (47 shorter events, 3.2 us)
Async XLA Ops:
  7.2 10.3 %copy-start = (f32[32,128,128]{2,1,0:T(8,128)S(1)}, f32[32,128,128]{2,1,0:T(8,128)}, u32[]{:S(2)}) copy-start(f32[32,128,128]{2,1,0:T(8,128)} %param.8) | copy-start | bytes 6291460
  10.0 13.9 %all-to-all-start = ((f32[8,2,5,4]{2,3,1,0:T(4,128)}), f32[8,2,5,4]{2,3,1,0:T(4,128)S(1)}, u32[]{:S(2)}, u32[]{:S(2)}) async-start(f32[8,2,5,4]{2,3,1,0:T(4,128)} %copy.16), calls=%async_computation | async-start | bytes 65536 | tf_op jit(solution)/shard_map/all_to_all | solution.py:269
  23.9 51.4 %all-to-all-start.1 = ((f32[8,4,128,128]{3,2,1,0:T(8,128)}), f32[8,4,128,128]{3,2,1,0:T(8,128)}, u32[]{:S(2)}, u32[]{:S(2)}) async-start(f32[8,4,128,128]{3,2,1,0:T(8,128)} %bitcast.35), calls=%async_computation.1 | async-start | bytes 4194304 | tf_op jit(solution)/shard_map/all_to_all | solution.py:269
  28.3 2.1 %copy-start.3 = (s32[64,2]{0,1:T(2,128)S(1)}, s32[64,2]{0,1:T(2,128)}, u32[]{:S(2)}) copy-start(s32[64,2]{0,1:T(2,128)} %param.14) | copy-start | bytes 1540
  75.4 52.2 %all-to-all-start.2 = ((f32[8,4,128,128]{3,2,1,0:T(8,128)}), f32[8,4,128,128]{3,2,1,0:T(8,128)}, u32[]{:S(2)}, u32[]{:S(2)}) async-start(f32[8,4,128,128]{3,2,1,0:T(8,128)} %bitcast.34), calls=%async_computation.2 | async-start | bytes 4194304 | tf_op jit(solution)/shard_map/all_to_all | solution.py:269
  79.7 98.0 %reduce-scatter.2.cloned.1.call-start = ((), (), s32[]{:S(2)}) async-start(), calls=%async_computation.5 | async-start | bytes 2949120 | tf_op jit(solution)/shard_map/reduce_scatter | solution.py:288
  94.0 2.4 %copy-start.4 = (f32[16]{0:T(128)S(1)}, f32[16]{0:T(128)}, u32[]{:S(2)}) copy-start(f32[16]{0:T(128)} %param.15) | copy-start | bytes 196
  145.5 0.7 copy-start.1
  145.5 0.7 copy-start.2
  146.9 10.1 %all-to-all-start.3 = ((f32[8,1,512]{2,1,0:T(1,128)}), f32[8,1,512]{2,1,0:T(1,128)S(1)}, u32[]{:S(2)}, u32[]{:S(2)}) async-start(f32[8,1,512]{2,1,0:T(1,128)} %reshape.287), calls=%async_computation.3 | async-start | bytes 32768 | tf_op jit(solution)/shard_map/all_to_all | solution.py:269
Sparse Core Ops, SparseCore 0:
  145.6 32.0 reduce-scatter.1
where the time goes:
time: 189 us
  waiting for transfers between devices  79.3 us (42%)
  Pallas kernels  50 us (26%)
  starting transfers between devices  19.5 us (10%)
  between operations  14.2 us (8%)
  other arithmetic  13.7 us (7%)
  local copies, waits for them, and re-layouts  11.7 us (6%)
    all_to_all x4, waiting for transfers between devices, body(): lax.all_to_all(x, 'cls', split_axis=0, concat_axis=0, tiled=True)  61.1 us
    pallas_call x2, Pallas kernels, owner_terms(): pl.pallas_call(functools.partial(owner_kernel, side), grid_spec=pltpu.Pre...  36 us
    all_to_all x4, starting transfers between devices, body(): lax.all_to_all(x, 'cls', split_axis=0, concat_axis=0, tiled=True)  19.5 us
    reduce_scatter x1, waiting for transfers between devices, body(): share = lax.psum_scatter(total, 'grp', scatter_dimension=0, tiled=True)  18.2 us
    pallas_call x1, Pallas kernels, reference_half(): pl.pallas_call(functools.partial(reference_half_kernel, side), grid=(coun...  10.1 us
    gather x2, local copies, waits for them, and re-layouts, body(): particles[source[h]].reshape(owners, chunk, side, side)  4.03 us
    pallas_call x1, Pallas kernels, finish(): pl.pallas_call(functools.partial(finish_kernel, side, contrast.shape[0]),...  3.95 us
  transfers between devices with their start and end apart: 5, of which 5 were waited for; matrix products, arithmetic and copies ran while one was open for 12% of the time, Pallas kernels for 15%

commit v1 on v0

--- a/solution.py
+++ b/solution.py
@@ -249,46 +249,62 @@
     shifts = shift_list.shape[0]
     owners = lax.axis_size("cls")
     capacity = max(2, 2 * part_rows // owners)
-    chunk = capacity // 2
+    last = max(1, capacity // 4)
+    chunks = (capacity - last, last)
+    starts = (0, owners * chunks[0])
     slot_total = owners * capacity
 
-    owner_of = class_of // class_local
-    before = jnp.arange(part_rows)[:, None] > jnp.arange(part_rows)[None, :]
-    rank = jnp.sum((before & (owner_of[:, None] == owner_of[None, :])).astype(jnp.int32), axis=1)
-    target = (rank // chunk) * (owners * chunk) + owner_of * chunk + rank % chunk
+    def places(classes):
+        owner = classes // class_local
+        rows = jnp.arange(part_rows)
+        before = rows[:, None] > rows[None, :]
+        same = owner[..., :, None] == owner[..., None, :]
+        return owner, jnp.sum((before & same).astype(jnp.int32), axis=-1)
+
+    owner_of, rank = places(class_of)
+    target = jnp.where(
+        rank < chunks[0],
+        owner_of * chunks[0] + rank,
+        starts[1] + owner_of * chunks[1] + rank - chunks[0],
+    )
     hit = target[None, :] == jnp.arange(slot_total, dtype=jnp.int32)[:, None]
-    values = jnp.stack(
-        [class_of % class_local, defocus_bin, shift_best, rotation_bin, jnp.ones_like(class_of)]
-    )
-    info = jnp.sum(jnp.where(hit[None], values[:, None, :], 0), axis=2).astype(f32)
-    source = jnp.sum(
-        jnp.where(hit, jnp.arange(part_rows, dtype=jnp.int32)[None, :], 0), axis=1
-    ).reshape(2, owners * chunk)
-    send = [particles[source[h]].reshape(owners, chunk, side, side) for h in (0, 1)]
+    source = jnp.sum(jnp.where(hit, jnp.arange(part_rows, dtype=jnp.int32)[None, :], 0), axis=1)
+    send = [
+        particles[source[s : s + owners * c]].reshape(owners, c, side, side)
+        for s, c in zip(starts, chunks)
+    ]
 
     exchange = lambda x: lax.all_to_all(x, "cls", split_axis=0, concat_axis=0, tiled=True)
-    info = info.reshape(5, 2, owners, chunk).transpose(2, 1, 0, 3)
-    got = [exchange(send[0])]
-    info = exchange(info).astype(jnp.int32).transpose(1, 2, 0, 3).reshape(2, 5, owners * chunk)
-    got.append(exchange(send[1]))
-
     right, left = dft_tables(side)
     contrast = contrast_half(defocus, side)
     phase, score_right, score_left = shift_tables(shift_list, side)
     tables = (contrast, phase, split_table(right), split_table(left), split_table(score_right), score_left)
     refs = reference_half(references)
+    got = [exchange(send[0])]
+    got[0], send[1], refs, tables = lax.optimization_barrier((got[0], send[1], refs, tables))
+    got.append(exchange(send[1]))
+
+    facts = jnp.stack([class_of, defocus_bin, shift_best, rotation_bin]).astype(f32)
+    facts = lax.all_gather(facts, "cls", axis=0).astype(jnp.int32).transpose(1, 0, 2)
+    from_owner, from_rank = places(facts[0])
+    mine = from_owner == lax.axis_index("cls")
+    values = jnp.stack([facts[0] % class_local, facts[1], facts[2], facts[3], jnp.ones_like(facts[0])])
+
+    def slot_info(first, count):
+        slot = first + jnp.arange(count, dtype=jnp.int32)
+        found = mine[:, None, :] & (from_rank[:, None, :] == slot[None, :, None])
+        return jnp.sum(jnp.where(found[None], values[:, :, None, :], 0), axis=-1).reshape(5, -1)
+
+    info = [slot_info(0, chunks[0]), slot_info(chunks[0], chunks[1])]
 
     total = jnp.zeros((class_local, 2 * HALF, side), f32)
     found = []
     for h in (0, 1):
-        scores, total = owner_terms(
-            got[h].reshape(owners * chunk, side, side), info[h], total, refs, tables
-        )
-        found.append(scores[:, :shifts].reshape(owners, chunk, shifts))
+        scores, total = owner_terms(got[h].reshape(-1, side, side), info[h], total, refs, tables)
+        found.append(scores[:, :shifts].reshape(owners, chunks[h], shifts))
     share = lax.psum_scatter(total, "grp", scatter_dimension=0, tiled=True)
-    home = exchange(jnp.concatenate(found, axis=1))
-    home = home.reshape(owners, 2, chunk, shifts).transpose(1, 0, 2, 3)
-    scores = home.reshape(slot_total, shifts)[target]
+    home = exchange(jnp.concatenate(found, axis=1)).reshape(slot_total, shifts)
+    scores = home[owner_of * capacity + rank]
     return scores, finish(share, contrast)
 
 

time: 189 us -> 221 us (1.17)
  blocking collectives: 0 us -> 87.5 us
  waiting for transfers between devices: 79.3 us -> 24.8 us
  starting transfers between devices: 19.5 us -> 17 us
    all_gather x0 -> x1, blocking collectives: none -> 87.5 us  [body(): lax.all_gather(facts, 'cls', axis=0).astype(jnp.int32).transpose(1, 0, 2)]
    all_to_all x4 -> x3, waiting for transfers between devices: 61.1 us -> 6.57 us  [body(): lax.all_to_all(x, 'cls', split_axis=0, concat_axis=0, tiled=True)]
    all_to_all x4 -> x3, starting transfers between devices: 19.5 us -> 16.9 us  [body(): lax.all_to_all(x, 'cls', split_axis=0, concat_axis=0, tiled=True)]
  transfers between devices with their start and end apart: 5 -> 4, of which waited for: 5 -> 2; matrix products, arithmetic and copies ran while one was open for 12% -> 10% of each run, Pallas kernels for 15% -> 15%
where the time goes in v1:
time: 221 us
  blocking collectives  87.5 us (40%)
  Pallas kernels  50 us (23%)
  waiting for transfers between devices  24.8 us (11%)
  starting transfers between devices  17 us (8%)
  other arithmetic  15.6 us (7%)
  between operations  14.3 us (6%)
  local copies, waits for them, and re-layouts  11.4 us (5%)
    all_gather x1, blocking collectives, body(): lax.all_gather(facts, 'cls', axis=0).astype(jnp.int32).transpose(1, 0, 2)  87.5 us
    pallas_call x2, Pallas kernels, owner_terms(): pl.pallas_call(functools.partial(owner_kernel, side), grid_spec=pltpu.Pre...  36 us
    reduce_scatter x1, waiting for transfers between devices, body(): share = lax.psum_scatter(total, 'grp', scatter_dimension=0, tiled=True)  18.2 us
    all_to_all x3, starting transfers between devices, body(): lax.all_to_all(x, 'cls', split_axis=0, concat_axis=0, tiled=True)  16.9 us
    pallas_call x1, Pallas kernels, reference_half(): pl.pallas_call(functools.partial(reference_half_kernel, side), grid=(coun...  10.1 us
    all_to_all x3, waiting for transfers between devices, body(): lax.all_to_all(x, 'cls', split_axis=0, concat_axis=0, tiled=True)  6.57 us
  transfers between devices with their start and end apart: 4, of which 2 were waited for; matrix products, arithmetic and copies ran while one was open for 10% of the time, Pallas kernels for 15%

profile of v1, /device:TPU:0, one launch (start us, length us, event | category | flops | bytes accessed | tf_op | source)
XLA Modules:
  0.0 220.6 jit_solution(885747496630651091)
XLA Ops:
  7.2 0.8 and_select_fusion.1
  8.2 0.7 compare_select_fusion.2
  9.0 2.5 %gather_fusion = f32[48,128,128]{2,1,0:T(8,128)} fusion(f32[32,128,128]{2,1,0:T(8,128)S(1)} %copy-done, s32[1024]{0:T(1024)S(1)} %pad_clamp_fusion.2), kind=kCustom, calls=%fused_computation | custom fusion | bytes 6291648 | tf_op jit(solution)/shard_map/gather | solution.py:273
  11.5 7.4 %all-to-all-start = ((f32[8,6,128,128]{3,2,1,0:T(8,128)}), f32[8,6,128,128]{3,2,1,0:T(8,128)}, u32[]{:S(2)}, u32[]{:S(2)}) async-start(f32[8,6,128,128]{3,2,1,0:T(8,128)} %bitcast.29), calls=%async_computation | async-start | bytes 6291456 | tf_op jit(solution)/shard_map/all_to_all | solution.py:277
  18.9 1.6 gather_fusion.1
  20.6 87.5 %all_gather.4 = f32[8,4,32]{2,1,0:T(4,128)S(1)} all-gather(f32[1,4,32]{2,1,0:T(4,128)S(1)} %add_convert_fusion), channel_id=1, replica_groups=mesh['grp'=4,'cls'=8] {'cls'}, dimensions={0}, use_global_device_ids=true | all-gather | bytes 4608 | tf_op jit(solution)/shard_map/all_gather | solution.py:288
  108.0 10.1 %reference_half.1.refs = f32[32,2,72,128]{3,2,1,0:T(8,128)} custom-call(f32[32,2,128,128]{3,2,1,0:T(8,128)} %ref.1), custom_call_target="tpu_custom_call" | custom-call | flops 603979776 | bytes 6553600 | tf_op jit(solution)/shard_map/reference_half/pallas_call | solution.py:125
  118.4 0.7 fusion.9
  119.3 0.7 maximum_maximum_fusion.score_left
  120.3 0.4 fusion.18
  121.0 0.8 fusion.7
  121.7 0.8 fusion.5
  123.0 1.3 multiply_subtract_fusion
  124.3 2.5 %pad_maximum_fusion.phase = f32[64,2,72,128]{3,2,1,0:T(8,128)} fusion(f32[64,1,72,128]{3,2,1,0:T(8,128)S(1)} %get-tuple-element.47, f32[64,1,72,128]{3,2,1,0:T(8,128)S(1)} %get-tuple-element.46), kind=kLoop, calls=%fused_computation.3 | loop fusion | flops 1179648 | bytes 9437184 | tf_op jit(solution)/shard_map/stack | solution.py:84
  126.8 3.2 %fusion.2.contrast = f32[16,72,128]{2,1,0:T(8,128)} fusion(f32[72,128]{1,0:T(8,128)S(1)} %add_multiply_fusion, f32[16]{0:T(128)S(1)} %copy-done.9), kind=kLoop, calls=%fused_computation.10 | loop fusion | flops 737280 | bytes 626752 | tf_op jit(solution)/shard_map/neg | solution.py:72
  129.9 3.6 %all-to-all-start.1 = ((f32[8,2,128,128]{3,2,1,0:T(8,128)}), f32[8,2,128,128]{3,2,1,0:T(8,128)S(1)}, u32[]{:S(2)}, u32[]{:S(2)}) async-start(f32[8,2,128,128]{3,2,1,0:T(8,128)} %bitcast.31), calls=%async_computation.1 | async-start | bytes 2097152 | tf_op jit(solution)/shard_map/all_to_all | solution.py:277
  134.5 0.7 copy.23.info
  135.2 0.6 select_reduce_fusion
  135.9 0.7 reshape.370.info
  136.6 1.6 broadcast_in_dim.75.start
  138.2 23.8 %owner_terms.2 = (f32[48,128]{1,0:T(8,128)}, f32[32,144,128]{2,1,0:T(8,128)}) custom-call(s32[5,48]{1,0:T(8,128)} %reshape.370.info, f32[48,128,128]{2,1,0:T(8,128)} %bitcast.14.images, f32[32,2,72,128]{3,2,1,0:T(8,128)} %reference_half.1.refs, f32[16,72,128]{2,1,0:T(8,128)} %fusion.2.contrast, f32[64,2,72,128]{3,2,1,0:T(8,128)} %pad_maximum_fusion.phase, ...), custom_call_target="tpu_custom_call" | custom-call | flops 3360000000 | bytes 17145728 | tf_op jit(solution)/shard_map/owner_terms/pallas_call | solution.py:186
  162.0 1.0 copy-done.1
  163.0 12.1 %owner_terms.3 = (f32[16,128]{1,0:T(8,128)}, f32[32,144,128]{2,1,0:T(8,128)}) custom-call(s32[5,16]{1,0:T(8,128)} %copy.23.info, f32[16,128,128]{2,1,0:T(8,128)} %bitcast.30, f32[32,2,72,128]{3,2,1,0:T(8,128)} %reference_half.1.refs, f32[16,72,128]{2,1,0:T(8,128)} %fusion.2.contrast, f32[64,2,72,128]{3,2,1,0:T(8,128)} %pad_maximum_fusion.phase, ...), custom_call_target="tpu_custom_call" | custom-call | flops 1120000000 | bytes 15048576 | tf_op jit(solution)/shard_map/owner_terms/pallas_call | solution.py:186
  175.1 0.7 copy-done.2
  175.9 0.7 reshape.407
  176.6 6.0 %all-to-all-start.2 = ((f32[8,1,512]{2,1,0:T(1,128)}), f32[8,1,512]{2,1,0:T(1,128)S(1)}, u32[]{:S(2)}, u32[]{:S(2)}) async-start(f32[8,1,512]{2,1,0:T(1,128)} %reshape.407), calls=%async_computation.2 | async-start | bytes 32768 | tf_op jit(solution)/shard_map/all_to_all | solution.py:277
  182.5 6.6 %all-to-all-done.2 = f32[8,1,512]{2,1,0:T(1,128)S(1)} async-done(((f32[8,1,512]{2,1,0:T(1,128)}), f32[8,1,512]{2,1,0:T(1,128)S(1)}, u32[]{:S(2)}, u32[]{:S(2)}) %all-to-all-start.2) | async-done | bytes 16416 | tf_op jit(solution)/shard_map/all_to_all | solution.py:277
  189.1 0.5 broadcast.584
  189.6 0.7 reduce
  190.4 1.2 gather_fusion.2
  191.5 18.2 %reduce-scatter.2.cloned.1.call-done.share = f32[8,144,128]{2,1,0:T(8,128)} async-done(((f32[32,144,128]{2,1,0:T(8,128)}), f32[8,144,128]{2,1,0:T(8,128)}) %reduce-scatter.2.cloned.1.call-update) | async-done | bytes 589840 | tf_op jit(solution)/shard_map/reduce_scatter | solution.py:305
  209.8 4.0 %finish.1 = f32[8,2,128,128]{3,2,1,0:T(8,128)} custom-call(f32[8,144,128]{2,1,0:T(8,128)} %reduce-scatter.2.cloned.1.call-done.share, f32[16,72,128]{2,1,0:T(8,128)} %fusion.2.contrast), custom_call_target="tpu_custom_call" | custom-call | flops 160000000 | bytes 4000000 | tf_op jit(solution)/shard_map/finish/pallas_call | solution.py:232
  (66 shorter events, 3.1 us)
Async XLA Ops:
  7.2 1.8 copy-start
  11.4 9.1 %copy-start.4 = (s32[32]{0:T(128)S(1)}, s32[32]{0:T(128)}, u32[]{:S(2)}) copy-start(s32[32]{0:T(128)} %param.10) | copy-start | bytes 388
  11.4 9.1 %copy-start.6 = (s32[32]{0:T(128)S(1)}, s32[32]{0:T(128)}, u32[]{:S(2)}) copy-start(s32[32]{0:T(128)} %param.11) | copy-start | bytes 388
  11.5 9.1 %copy-start.7 = (s32[32]{0:T(128)S(1)}, s32[32]{0:T(128)}, u32[]{:S(2)}) copy-start(s32[32]{0:T(128)} %param.12) | copy-start | bytes 388
  11.5 9.1 %copy-start.8 = (s32[32]{0:T(128)S(1)}, s32[32]{0:T(128)}, u32[]{:S(2)}) copy-start(s32[32]{0:T(128)} %param.13) | copy-start | bytes 388
  11.5 118.5 %all-to-all-start = ((f32[8,6,128,128]{3,2,1,0:T(8,128)}), f32[8,6,128,128]{3,2,1,0:T(8,128)}, u32[]{:S(2)}, u32[]{:S(2)}) async-start(f32[8,6,128,128]{3,2,1,0:T(8,128)} %bitcast.29), calls=%async_computation | async-start | bytes 6291456 | tf_op jit(solution)/shard_map/all_to_all | solution.py:277
  108.0 10.1 %copy-start.5 = (s32[64,2]{0,1:T(2,128)S(1)}, s32[64,2]{0,1:T(2,128)}, u32[]{:S(2)}) copy-start(s32[64,2]{0,1:T(2,128)} %param.14) | copy-start | bytes 1540
  124.3 2.5 %copy-start.9 = (f32[16]{0:T(128)S(1)}, f32[16]{0:T(128)}, u32[]{:S(2)}) copy-start(f32[16]{0:T(128)} %param.15) | copy-start | bytes 196
  129.9 32.0 %all-to-all-start.1 = ((f32[8,2,128,128]{3,2,1,0:T(8,128)}), f32[8,2,128,128]{3,2,1,0:T(8,128)S(1)}, u32[]{:S(2)}, u32[]{:S(2)}) async-start(f32[8,2,128,128]{3,2,1,0:T(8,128)} %bitcast.31), calls=%async_computation.1 | async-start | bytes 2097152 | tf_op jit(solution)/shard_map/all_to_all | solution.py:277
  133.5 76.3 %reduce-scatter.2.cloned.1.call-start = ((), (), s32[]{:S(2)}) async-start(), calls=%async_computation.4 | async-start | bytes 2949120 | tf_op jit(solution)/shard_map/reduce_scatter | solution.py:305
  162.0 1.0 copy-start.1
  175.1 0.7 copy-start.2
  175.1 0.7 copy-start.3
  176.6 12.6 %all-to-all-start.2 = ((f32[8,1,512]{2,1,0:T(1,128)}), f32[8,1,512]{2,1,0:T(1,128)S(1)}, u32[]{:S(2)}, u32[]{:S(2)}) async-start(f32[8,1,512]{2,1,0:T(1,128)} %reshape.407), calls=%async_computation.2 | async-start | bytes 32768 | tf_op jit(solution)/shard_map/all_to_all | solution.py:277
Sparse Core Ops, SparseCore 0:
  175.3 34.4 reduce-scatter.1

commit v2 on v1

--- a/solution.py
+++ b/solution.py
@@ -145,14 +145,17 @@
     def _():
         total[...] = start[...]
 
-    base = pl.program_id(0) * GROUP
+    group = scores.shape[1]
+    per_source = group // images.shape[0]
+    base = pl.program_id(0) * group
     lane = lax.broadcasted_iota(jnp.int32, (8, side), 1)
     tail_row = lax.broadcasted_iota(jnp.int32, (8, side), 0)
     rows = []
-    for n in range(GROUP):
+    for n in range(group):
         local, bin_at, shift = info[0, base + n], info[1, base + n], info[2, base + n]
         turns, live = info[3, base + n], info[4, base + n].astype(f32)
-        image = images[n]
+        at = n % per_source * side
+        image = images[n // per_source, at : at + side]
         image = jnp.where(turns % 2 == 1, image.T, image)
         right_at = (turns >= 2).astype(jnp.int32)
         left_at = ((turns == 1) | (turns == 2)).astype(jnp.int32)
@@ -172,11 +175,15 @@
         total[local, side // 2 : HALF] += tail
         total[local, HALF:] += con_im
     found = jnp.concatenate(rows, axis=0)
-    scores[...] = found + pltpu.roll(found, found.shape[1] // 2, 1)
+    scores[0] = found + pltpu.roll(found, found.shape[1] // 2, 1)
 
 
 def owner_terms(images, info, start, refs, tables):
-    count, side, _ = images.shape
+    sources, held, side = images.shape
+    per_source = held // side
+    count = sources * per_source
+    block = math.gcd(sources, max(1, GROUP // per_source))
+    group = block * per_source
     contrast, phase, right, left, score_right, score_left = tables
     whole = lambda x: pl.BlockSpec(
         x.shape, lambda i, info: (0,) * x.ndim, pipeline_mode=pl.Buffered(1)
@@ -187,16 +194,16 @@
         functools.partial(owner_kernel, side),
         grid_spec=pltpu.PrefetchScalarGridSpec(
             num_scalar_prefetch=1,
-            grid=(count // GROUP,),
-            in_specs=[pl.BlockSpec((GROUP, side, side), lambda i, info: (i, 0, 0))]
+            grid=(sources // block,),
+            in_specs=[pl.BlockSpec((block, held, side), lambda i, info: (i, 0, 0))]
             + [whole(x) for x in fixed],
             out_specs=[
-                pl.BlockSpec((GROUP, lanes), lambda i, info: (i, 0)),
+                pl.BlockSpec((1, group, lanes), lambda i, info: (i, 0, 0)),
                 pl.BlockSpec(start.shape, lambda i, info: (0, 0, 0)),
             ],
         ),
         out_shape=[
-            jax.ShapeDtypeStruct((count, lanes), f32),
+            jax.ShapeDtypeStruct((sources // block, group, lanes), f32),
             jax.ShapeDtypeStruct(start.shape, f32),
         ],
         compiler_params=pltpu.CompilerParams(vmem_limit_bytes=VMEM_BYTES),
@@ -208,36 +215,127 @@
     )(info, images, *fixed)
 
 
-def finish_kernel(side, bins, share, contrast, out):
+def finish_class(side, bins, share, contrast, out, n):
     row_pick = mirror_pick(side // 2, HALF, side, side // 2)
     col_pick = mirror_pick(side, side, side, 0)
     tail_row = lax.broadcasted_iota(jnp.int32, (8, side), 0)
     middle = side // 2
-    for n in range(share.shape[0]):
-        counts = share[n, middle + 1 : middle + 2]
-        weight = jnp.ones((HALF, side), f32)
-        for d in range(bins):
-            weight += counts[:, d : d + 1] * (contrast[d] * contrast[d])
-        live = lax.broadcasted_iota(jnp.int32, (HALF, side), 0) <= middle
-        for part, sign in ((0, 1.0), (1, -1.0)):
-            fresh = jnp.where(live, share[n, part * HALF : (part + 1) * HALF], 0.0) / weight
-            other = sign * mirrored(fresh, row_pick, col_pick)
-            out[n, part, :middle] = fresh[:middle]
-            out[n, part, middle : middle + 8] = jnp.where(tail_row == 0, fresh[middle:], other[:8])
-            out[n, part, middle + 8 :] = other[8:]
-
-
-def finish(share, contrast):
-    count, _, side = share.shape
+    counts = share[middle + 1 : middle + 2]
+    weight = jnp.ones((HALF, side), f32)
+    for d in range(bins):
+        weight += counts[:, d : d + 1] * (contrast[d] * contrast[d])
+    live = lax.broadcasted_iota(jnp.int32, (HALF, side), 0) <= middle
+    for part, sign in ((0, 1.0), (1, -1.0)):
+        fresh = jnp.where(live, share[part * HALF : (part + 1) * HALF], 0.0) / weight
+        other = sign * mirrored(fresh, row_pick, col_pick)
+        out[n, part, :middle] = fresh[:middle]
+        out[n, part, middle : middle + 8] = jnp.where(tail_row == 0, fresh[middle:], other[:8])
+        out[n, part, middle + 8 :] = other[8:]
+
+
+def close_kernel(
+    side, bins, groups, owners, total, found, contrast, out, home,
+    near, mid, far, board, near_send, near_recv, far_send, far_recv, score_send, score_recv,
+):
+    mesh_ids = pl.DeviceIdType.MESH
+    grp, cls = lax.axis_index("grp"), lax.axis_index("cls")
+    row, core = grp // 2, grp % 2
+    rows = groups // 2
+    pieces = near_send.shape[1]
+    per = total.shape[2]
+    size = per // pieces
+    partner = 2 * row + (1 - core)
+    row_at = [lax.rem(row + d, rows) for d in range(rows)]
+    cls_at = [lax.rem(cls + d, owners) for d in range(owners)]
+
+    barrier = pltpu.get_barrier_semaphore()
+    greet = [{"grp": partner}] + [{"grp": 2 * row_at[d] + core} for d in range(1, rows)]
+    greet += [{"cls": cls_at[d]} for d in range(1, owners)]
+    for device in greet:
+        pl.semaphore_signal(barrier, inc=1, device_id=device, device_id_type=mesh_ids)
+    pl.semaphore_wait(barrier, len(greet))
+
+    def copy(source, target, send, recv, device):
+        made = pltpu.make_async_remote_copy(
+            src_ref=source, dst_ref=target, send_sem=send, recv_sem=recv,
+            device_id=device, device_id_type=mesh_ids,
+        )
+        made.start()
+        return made
+
+    order = [(d, q) for d in list(range(1, rows)) + [0] for q in range(pieces)]
+    near_copies, far_copies = {}, {}
+    for d, q in order:
+        span = pl.ds(q * size, size)
+        near_copies[d, q] = copy(
+            total.at[row_at[d], 1 - core, span], near.at[d, span],
+            near_send.at[d, q], near_recv.at[d, q], {"grp": partner},
+        )
+    for d, q in order:
+        near_copies[d, q].wait()
+        if d == 0:
+            continue
+        span = pl.ds(q * size, size)
+        mid[d - 1, span] = total[row_at[d], core, span] + near[d, span]
+        far_copies[d, q] = copy(
+            mid.at[d - 1, span], far.at[d - 1, span],
+            far_send.at[d - 1, q], far_recv.at[d - 1, q], {"grp": 2 * row_at[d] + core},
+        )
+    score_copies = [
+        copy(
+            found.at[cls_at[d]], board.at[cls],
+            score_send.at[d], score_recv.at[d], {"cls": cls_at[d]},
+        )
+        for d in range(1, owners)
+    ]
+    for q in range(pieces):
+        for d in range(1, rows):
+            far_copies[d, q].wait()
+        for n in range(q * size, (q + 1) * size):
+            share = total[row, core, n] + near[0, n]
+            for d in range(1, rows):
+                share = share + far[d - 1, n]
+            finish_class(side, bins, share, contrast, out, n)
+    for made in score_copies:
+        made.wait()
+    board[cls] = found[cls]
+    home[...] = board[...]
+
+
+def close(total, found, contrast, groups, owners):
+    class_local, height, side = total.shape
+    rows, per = groups // 2, class_local // groups
+    pieces = math.gcd(per, 2)
+    dma = pltpu.SemaphoreType.DMA
+    vmem = pl.BlockSpec(memory_space=pltpu.VMEM)
     return pl.pallas_call(
-        functools.partial(finish_kernel, side, contrast.shape[0]),
-        out_shape=jax.ShapeDtypeStruct((count, 2, side, side), f32),
-        compiler_params=pltpu.CompilerParams(vmem_limit_bytes=VMEM_BYTES),
+        functools.partial(close_kernel, side, contrast.shape[0], groups, owners),
+        in_specs=[vmem] * 3,
+        out_specs=[vmem] * 2,
+        out_shape=[
+            jax.ShapeDtypeStruct((per, 2, side, side), f32),
+            jax.ShapeDtypeStruct(found.shape, f32),
+        ],
+        scratch_shapes=[
+            pltpu.VMEM((rows, per, height, side), f32),
+            pltpu.VMEM((max(1, rows - 1), per, height, side), f32),
+            pltpu.VMEM((max(1, rows - 1), per, height, side), f32),
+            pltpu.VMEM(found.shape, f32),
+            dma((rows, pieces)),
+            dma((rows, pieces)),
+            dma((max(1, rows - 1), pieces)),
+            dma((max(1, rows - 1), pieces)),
+            dma((owners,)),
+            dma((owners,)),
+        ],
+        compiler_params=pltpu.CompilerParams(
+            collective_id=0, has_side_effects=True, vmem_limit_bytes=VMEM_BYTES
+        ),
         cost_estimate=pl.CostEstimate(
-            flops=count * 20_000_000, bytes_accessed=4_000_000, transcendentals=0
-        ),
-        name="finish",
-    )(share, contrast)
+            flops=per * 20_000_000, bytes_accessed=8_000_000, transcendentals=0
+        ),
+        name="close",
+    )(total.reshape(rows, 2, per, height, side), found, contrast)
 
 
 def body(
@@ -270,9 +368,17 @@
     hit = target[None, :] == jnp.arange(slot_total, dtype=jnp.int32)[:, None]
     source = jnp.sum(jnp.where(hit, jnp.arange(part_rows, dtype=jnp.int32)[None, :], 0), axis=1)
     send = [
-        particles[source[s : s + owners * c]].reshape(owners, c, side, side)
+        particles[source[s : s + owners * c]].reshape(owners, c * side, side)
         for s, c in zip(starts, chunks)
     ]
+    facts = jnp.stack(
+        [class_of % class_local, defocus_bin, shift_best, rotation_bin, jnp.ones_like(class_of)]
+    )
+    place = (owner_of * capacity + rank)[None, :] == jnp.arange(slot_total, dtype=jnp.int32)[:, None]
+    facts = jnp.sum(jnp.where(place[None], facts[:, None, :], 0), axis=2).astype(f32)
+    facts = facts.reshape(5, owners, capacity).transpose(1, 0, 2)
+    facts = jnp.pad(facts, ((0, 0), (0, 3), (0, side - capacity)))
+    send[0] = jnp.concatenate([send[0], facts], axis=1)
 
     exchange = lambda x: lax.all_to_all(x, "cls", split_axis=0, concat_axis=0, tiled=True)
     right, left = dft_tables(side)
@@ -284,28 +390,22 @@
     got[0], send[1], refs, tables = lax.optimization_barrier((got[0], send[1], refs, tables))
     got.append(exchange(send[1]))
 
-    facts = jnp.stack([class_of, defocus_bin, shift_best, rotation_bin]).astype(f32)
-    facts = lax.all_gather(facts, "cls", axis=0).astype(jnp.int32).transpose(1, 0, 2)
-    from_owner, from_rank = places(facts[0])
-    mine = from_owner == lax.axis_index("cls")
-    values = jnp.stack([facts[0] % class_local, facts[1], facts[2], facts[3], jnp.ones_like(facts[0])])
-
-    def slot_info(first, count):
-        slot = first + jnp.arange(count, dtype=jnp.int32)
-        found = mine[:, None, :] & (from_rank[:, None, :] == slot[None, :, None])
-        return jnp.sum(jnp.where(found[None], values[:, :, None, :], 0), axis=-1).reshape(5, -1)
-
-    info = [slot_info(0, chunks[0]), slot_info(chunks[0], chunks[1])]
+    facts = got[0][:, chunks[0] * side : chunks[0] * side + 5, :capacity].astype(jnp.int32)
+    facts = facts.transpose(1, 0, 2)
+    info = [
+        facts[:, :, : chunks[0]].reshape(5, -1),
+        facts[:, :, chunks[0] :].reshape(5, -1),
+    ]
 
     total = jnp.zeros((class_local, 2 * HALF, side), f32)
     found = []
     for h in (0, 1):
-        scores, total = owner_terms(got[h].reshape(-1, side, side), info[h], total, refs, tables)
-        found.append(scores[:, :shifts].reshape(owners, chunks[h], shifts))
-    share = lax.psum_scatter(total, "grp", scatter_dimension=0, tiled=True)
-    home = exchange(jnp.concatenate(found, axis=1)).reshape(slot_total, shifts)
-    scores = home[owner_of * capacity + rank]
-    return scores, finish(share, contrast)
+        scores, total = owner_terms(got[h], info[h], total, refs, tables)
+        found.append(scores.reshape(owners, chunks[h], -1))
+    found = jnp.concatenate(found, axis=1)
+    fresh, home = close(total, found, contrast, lax.axis_size("grp"), owners)
+    home = home.reshape(slot_total, -1)
+    return home[owner_of * capacity + rank][:, :shifts], fresh
 
 
 def solution(mesh):

time: 221 us -> 165 us (0.75)
  blocking collectives: 87.5 us -> 0 us
  waiting for transfers between devices: 24.8 us -> 48 us
  Pallas kernels: 50 us -> 72.6 us
  between operations: 14.3 us -> 0.83 us
  starting transfers between devices: 17 us -> 10.9 us
  other arithmetic: 15.6 us -> 19 us
    all_gather x1 -> x0, blocking collectives: 87.5 us -> none  [body(): lax.all_gather(facts, 'cls', axis=0).astype(jnp.int32).transpose(1, 0, 2)]
    all_to_all x3 -> x2, waiting for transfers between devices: 6.57 us -> 48 us  [body(): lax.all_to_all(x, 'cls', split_axis=0, concat_axis=0, tiled=True)]
    pallas_call x1, Pallas kernels: 3.96 us -> 25.4 us  [close(): pl.pallas_call(functools.partial(close_kernel, side, contrast.shape[0], g...]
    reduce_scatter x1 -> x0, waiting for transfers between devices: 18.2 us -> none  [body(): share = lax.psum_scatter(total, 'grp', scatter_dimension=0, tiled=True)]
    all_to_all x3 -> x2, starting transfers between devices: 16.9 us -> 10.9 us  [body(): lax.all_to_all(x, 'cls', split_axis=0, concat_axis=0, tiled=True)]
    concatenate x1 -> x2, other arithmetic: 0.01 us -> 5.18 us  [the longest x1 3.85 us: body(): send[0] = jnp.concatenate([send[0], facts], axis=1)]
  transfers between devices with their start and end apart: 4 -> 2, of which waited for: 2 -> 1; matrix products, arithmetic and copies ran while one was open for 10% -> 10% of each run, Pallas kernels for 15% -> 21%
where the time goes in v2:
time: 165 us; the launch traced here: 164 us
  Pallas kernels  72.6 us (44%)
  waiting for transfers between devices  48 us (29%)
  other arithmetic  19 us (12%)
  local copies, waits for them, and re-layouts  13.1 us (8%)
  starting transfers between devices  10.9 us (7%)
    all_to_all x2, waiting for transfers between devices, body(): lax.all_to_all(x, 'cls', split_axis=0, concat_axis=0, tiled=True)  48 us
    pallas_call x2, Pallas kernels, owner_terms(): pl.pallas_call(functools.partial(owner_kernel, side), grid_spec=pltpu.Pre...  37.1 us
    pallas_call x1, Pallas kernels, close(): pl.pallas_call(functools.partial(close_kernel, side, contrast.shape[0], g...  25.4 us
    all_to_all x2, starting transfers between devices, body(): lax.all_to_all(x, 'cls', split_axis=0, concat_axis=0, tiled=True)  10.9 us
    pallas_call x1, Pallas kernels, reference_half(): pl.pallas_call(functools.partial(reference_half_kernel, side), grid=(coun...  10 us
    gather x2, local copies, waits for them, and re-layouts, body(): particles[source[s:s + owners * c]].reshape(owners, c * side, side)  3.98 us
    concatenate x1, other arithmetic, body(): send[0] = jnp.concatenate([send[0], facts], axis=1)  3.85 us
  transfers between devices with their start and end apart: 2, of which 1 were waited for; matrix products, arithmetic and copies ran while one was open for 10% of the time, Pallas kernels for 21%

profile of v2, /device:TPU:0, one launch (start us, length us, event | category | flops | bytes accessed | tf_op | source)
XLA Modules:
  0.0 164.4 jit_solution(4054911998107793003)
XLA Ops:
  0.6 0.8 and_select_fusion.1
  1.7 0.7 stack.42
  2.8 2.4 %gather_fusion = f32[48,128,128]{2,1,0:T(8,128)} fusion(f32[32,128,128]{2,1,0:T(8,128)S(1)} %copy-done, s32[1024]{0:T(1024)S(1)} %pad_clamp_fusion.2), kind=kCustom, calls=%fused_computation | custom fusion | bytes 6291648 | tf_op jit(solution)/shard_map/gather | solution.py:371
  5.2 3.9 %select_maximum_fusion = f32[8,776,128]{2,1,0:T(8,128)} fusion(f32[8,5,8]{2,1,0:T(8,128)S(1)} %bitcast.35, f32[8,768,128]{2,1,0:T(8,128)} %bitcast.30), kind=kLoop, calls=%fused_computation.4 | loop fusion | flops 2383872 | bytes 6325504 | tf_op jit(solution)/shard_map/concatenate | solution.py:381
  9.0 7.3 %all-to-all-start = ((f32[8,776,128]{2,1,0:T(8,128)}), f32[8,776,128]{2,1,0:T(8,128)}, u32[]{:S(2)}, u32[]{:S(2)}) async-start(f32[8,776,128]{2,1,0:T(8,128)} %select_maximum_fusion), calls=%async_computation | async-start | bytes 6356992 | tf_op jit(solution)/shard_map/all_to_all | solution.py:383
  16.4 1.6 gather_fusion.1
  17.9 10.0 %reference_half.1.refs = f32[32,2,72,128]{3,2,1,0:T(8,128)} custom-call(f32[32,2,128,128]{3,2,1,0:T(8,128)} %ref.1), custom_call_target="tpu_custom_call" | custom-call | flops 603979776 | bytes 6553600 | tf_op jit(solution)/shard_map/reference_half/pallas_call | solution.py:125
  28.1 0.3 fusion.48
  28.3 0.7 fusion.9
  29.2 0.7 maximum_maximum_fusion.score_left
  29.9 0.3 sine_multiply_fusion.1
  30.2 0.4 fusion.18
  30.8 0.8 fusion.7
  31.6 0.8 fusion.5
  32.4 0.2 fusion.56
  32.7 0.2 fusion.58
  32.9 1.3 multiply_subtract_fusion
  34.2 2.5 %pad_maximum_fusion.phase = f32[64,2,72,128]{3,2,1,0:T(8,128)} fusion(f32[64,1,72,128]{3,2,1,0:T(8,128)S(1)} %get-tuple-element.51, f32[64,1,72,128]{3,2,1,0:T(8,128)S(1)} %get-tuple-element.50), kind=kLoop, calls=%fused_computation.3 | loop fusion | flops 1179648 | bytes 9437184 | tf_op jit(solution)/shard_map/stack | solution.py:84
  36.6 3.2 %fusion.2.contrast = f32[16,72,128]{2,1,0:T(8,128)} fusion(f32[72,128]{1,0:T(8,128)S(1)} %add_multiply_fusion, f32[16]{0:T(128)S(1)} %copy-done.4), kind=kLoop, calls=%fused_computation.12 | loop fusion | flops 737280 | bytes 626752 | tf_op jit(solution)/shard_map/neg | solution.py:72
  39.8 48.0 %all-to-all-done.images = f32[8,776,128]{2,1,0:T(8,128)} async-done(((f32[8,776,128]{2,1,0:T(8,128)}), f32[8,776,128]{2,1,0:T(8,128)}, u32[]{:S(2)}, u32[]{:S(2)}) %all-to-all-start) | async-done | bytes 3178528 | tf_op jit(solution)/shard_map/all_to_all | solution.py:383
  87.8 3.6 %all-to-all-start.1 = ((f32[8,256,128]{2,1,0:T(8,128)}), f32[8,256,128]{2,1,0:T(8,128)S(1)}, u32[]{:S(2)}, u32[]{:S(2)}) async-start(f32[8,256,128]{2,1,0:T(8,128)} %bitcast.31), calls=%async_computation.1 | async-start | bytes 2097152 | tf_op jit(solution)/shard_map/all_to_all | solution.py:383
  91.4 0.8 convert_bitcast_fusion
  92.4 0.7 copy.19.info
  93.1 0.7 reshape.243.info
  93.8 1.5 broadcast_in_dim.95.start
  95.3 24.9 %owner_terms.2 = (f32[8,6,128]{2,1,0:T(8,128)}, f32[32,144,128]{2,1,0:T(8,128)}) custom-call(s32[5,48]{1,0:T(8,128)} %reshape.243.info, f32[8,776,128]{2,1,0:T(8,128)} %all-to-all-done.images, f32[32,2,72,128]{3,2,1,0:T(8,128)} %reference_half.1.refs, f32[16,72,128]{2,1,0:T(8,128)} %fusion.2.contrast, f32[64,2,72,128]{3,2,1,0:T(8,128)} %pad_maximum_fusion.phase, ...), custom_call_target="tpu_custom_call" | custom-call | flops 3360000000 | bytes 17145728 | tf_op jit(solution)/shard_map/owner_terms/pallas_call | solution.py:193
  120.2 1.0 copy-done.1
  121.1 12.3 %owner_terms.3 = (f32[2,8,128]{2,1,0:T(8,128)}, f32[32,144,128]{2,1,0:T(8,128)}) custom-call(s32[5,16]{1,0:T(8,128)} %copy.19.info, f32[8,256,128]{2,1,0:T(8,128)} %copy-done.1, f32[32,2,72,128]{3,2,1,0:T(8,128)} %reference_half.1.refs, f32[16,72,128]{2,1,0:T(8,128)} %fusion.2.contrast, f32[64,2,72,128]{3,2,1,0:T(8,128)} %pad_maximum_fusion.phase, ...), custom_call_target="tpu_custom_call" | custom-call | flops 1120000000 | bytes 15048576 | tf_op jit(solution)/shard_map/owner_terms/pallas_call | solution.py:193
  133.4 1.3 pad_maximum_fusion.4.found
  134.7 25.4 %close.1 = (f32[8,2,128,128]{3,2,1,0:T(8,128)}, f32[8,8,128]{2,1,0:T(8,128)}) custom-call(f32[2,2,8,144,128]{4,3,2,1,0:T(8,128)} %bitcast.32, f32[8,8,128]{2,1,0:T(8,128)} %pad_maximum_fusion.4.found, f32[16,72,128]{2,1,0:T(8,128)} %fusion.2.contrast), custom_call_target="tpu_custom_call" | custom-call | flops 160000000 | bytes 8000000 | tf_op jit(solution)/shard_map/close/pallas_call | solution.py:311
  160.2 1.9 %gather_fusion.2 = f32[32,128]{1,0:T(8,128)} fusion(f32[64,128]{1,0:T(8,128)} %bitcast.33, s32[1024]{0:T(1024)S(1)} %pad_clamp_fusion), kind=kCustom, calls=%fused_computation.2 | custom fusion | bytes 32896 | tf_op jit(solution)/shard_map/gather | solution.py:408
  162.1 2.3 %copy.23 = f32[8,2,128,128]{3,2,1,0:T(8,128)} copy(f32[8,2,128,128]{3,2,1,0:T(8,128)} %get-tuple-element.80) | data formatting | bytes 2097152
  (41 shorter events, 1.4 us)
Async XLA Ops:
  0.6 2.1 %copy-start = (f32[32,128,128]{2,1,0:T(8,128)S(1)}, f32[32,128,128]{2,1,0:T(8,128)}, u32[]{:S(2)}) copy-start(f32[32,128,128]{2,1,0:T(8,128)} %param.8) | copy-start | bytes 6291460
  9.0 78.8 %all-to-all-start = ((f32[8,776,128]{2,1,0:T(8,128)}), f32[8,776,128]{2,1,0:T(8,128)}, u32[]{:S(2)}, u32[]{:S(2)}) async-start(f32[8,776,128]{2,1,0:T(8,128)} %select_maximum_fusion), calls=%async_computation | async-start | bytes 6356992 | tf_op jit(solution)/shard_map/all_to_all | solution.py:383
  17.9 10.1 %copy-start.3 = (s32[64,2]{0,1:T(2,128)S(1)}, s32[64,2]{0,1:T(2,128)}, u32[]{:S(2)}) copy-start(s32[64,2]{0,1:T(2,128)} %param.14) | copy-start | bytes 1540
  34.2 2.5 %copy-start.4 = (f32[16]{0:T(128)S(1)}, f32[16]{0:T(128)}, u32[]{:S(2)}) copy-start(f32[16]{0:T(128)} %param.15) | copy-start | bytes 196
  87.8 32.4 %all-to-all-start.1 = ((f32[8,256,128]{2,1,0:T(8,128)}), f32[8,256,128]{2,1,0:T(8,128)S(1)}, u32[]{:S(2)}, u32[]{:S(2)}) async-start(f32[8,256,128]{2,1,0:T(8,128)} %bitcast.31), calls=%async_computation.1 | async-start | bytes 2097152 | tf_op jit(solution)/shard_map/all_to_all | solution.py:383
  120.2 1.0 copy-start.1
  121.1 12.3 %copy-start.2 = (f32[8,6,128]{2,1,0:T(8,128)S(1)}, f32[8,6,128]{2,1,0:T(8,128)}, u32[]{:S(2)}) copy-start(f32[8,6,128]{2,1,0:T(8,128)} %get-tuple-element.34) | copy-start | bytes 73732

commit v3 on v2

--- a/solution.py
+++ b/solution.py
@@ -108,54 +108,69 @@
     return total
 
 
-def reference_half_kernel(side, ref, out):
+def gather_kernel(
+    side, owners, chunks, info, last, send, references, phase_in, contrast,
+    right_hi, right_lo, left_hi, left_lo, sr_hi, sr_lo, score_left, scores, total,
+    got, held_refs, phase, refs, running, send_sem, recv_sem, local_sem,
+):
+    mesh_ids = pl.DeviceIdType.MESH
+    cls = lax.axis_index("cls")
+    slots = scores.shape[2]
+    span = slots * side
+    classes = refs.shape[0]
+
+    local_copies = [
+        pltpu.make_async_copy(references, held_refs, local_sem.at[0]),
+        pltpu.make_async_copy(phase_in, phase, local_sem.at[1]),
+        pltpu.make_async_copy(send.at[cls], got.at[cls], local_sem.at[2]),
+    ]
+
+    def copy(r, d):
+        to = lax.rem(cls + d, owners)
+        rows = pl.ds(pl.multiple_of(r * span, side), span)
+        return pltpu.make_async_remote_copy(
+            src_ref=send.at[to, rows], dst_ref=got.at[cls, rows],
+            send_sem=send_sem.at[r, d], recv_sem=recv_sem.at[r, d],
+            device_id={"cls": to}, device_id_type=mesh_ids,
+        )
+
+    barrier = pltpu.get_barrier_semaphore()
+    for d in range(1, owners):
+        pl.semaphore_signal(
+            barrier, inc=1, device_id={"cls": lax.rem(cls + d, owners)}, device_id_type=mesh_ids
+        )
+    for made in local_copies:
+        made.start()
+    pl.semaphore_wait(barrier, owners - 1)
+    for r in range(min(2, chunks)):
+        for d in range(1, owners):
+            copy(r, d).start()
+
+    running[0] = jnp.zeros(running.shape[1:], f32)
+    for made in local_copies:
+        made.wait()
     row_pick = mirror_pick(HALF, side, side, 0)
     col_pick = mirror_pick(side, side, side, 0)
-    live = lax.broadcasted_iota(jnp.int32, (HALF, side), 0) <= side // 2
-    for n in range(ref.shape[0]):
-        for part, sign in ((0, 1.0), (1, -1.0)):
-            x = ref[n, part]
-            both = 0.5 * (x[:HALF] + sign * mirrored(x, row_pick, col_pick))
-            out[n, part] = jnp.where(live, both, 0.0)
-
-
-def reference_half(references):
-    count, _, side, _ = references.shape
-    step = math.gcd(count, 4)
-    return pl.pallas_call(
-        functools.partial(reference_half_kernel, side),
-        grid=(count // step,),
-        in_specs=[pl.BlockSpec((step, 2, side, side), lambda i: (i, 0, 0, 0))],
-        out_specs=pl.BlockSpec((step, 2, HALF, side), lambda i: (i, 0, 0, 0)),
-        out_shape=jax.ShapeDtypeStruct((count, 2, HALF, side), f32),
-        compiler_params=pltpu.CompilerParams(vmem_limit_bytes=VMEM_BYTES),
-        cost_estimate=pl.CostEstimate(
-            flops=count * 2 * 8 * HALF * side * side, bytes_accessed=count * 4 * 200 * side * 2,
-            transcendentals=0,
-        ),
-        name="reference_half",
-    )(references)
-
-
-def owner_kernel(
-    side, info, images, refs, contrast, phase, right_hi, right_lo, left_hi, left_lo,
-    sr_hi, sr_lo, score_left, start, scores, total,
-):
-    @pl.when(pl.program_id(0) == 0)
-    def _():
-        total[...] = start[...]
-
-    group = scores.shape[1]
-    per_source = group // images.shape[0]
-    base = pl.program_id(0) * group
+    live_row = lax.broadcasted_iota(jnp.int32, (HALF, side), 0) <= side // 2
+    at_once = math.gcd(classes, 4)
+
+    def halve(step, carry):
+        for n in range(at_once):
+            for part, sign in ((0, 1.0), (1, -1.0)):
+                x = held_refs[step * at_once + n, part]
+                both = 0.5 * (x[:HALF] + sign * mirrored(x, row_pick, col_pick))
+                refs[step * at_once + n, part] = jnp.where(live_row, both, 0.0)
+        return carry
+
+    lax.fori_loop(0, classes // at_once, halve, 0)
+
     lane = lax.broadcasted_iota(jnp.int32, (8, side), 1)
     tail_row = lax.broadcasted_iota(jnp.int32, (8, side), 0)
-    rows = []
-    for n in range(group):
-        local, bin_at, shift = info[0, base + n], info[1, base + n], info[2, base + n]
-        turns, live = info[3, base + n], info[4, base + n].astype(f32)
-        at = n % per_source * side
-        image = images[n // per_source, at : at + side]
+    block = math.gcd(owners, max(1, GROUP // slots))
+
+    def particle(at, image):
+        bin_at, shift = info[1, at], info[2, at]
+        local, turns, live = info[0, at], info[3, at], info[4, at].astype(f32)
         image = jnp.where(turns % 2 == 1, image.T, image)
         right_at = (turns >= 2).astype(jnp.int32)
         left_at = ((turns == 1) | (turns == 2)).astype(jnp.int32)
@@ -167,52 +182,87 @@
         ref_re, ref_im = refs[local, 0], refs[local, 1]
         product = jnp.concatenate([re * ref_re + im * ref_im, im * ref_re - re * ref_im], axis=0)
         part = dot3(split(product), (sr_hi[...], sr_lo[...]))
-        rows.append(jnp.sum(part * score_left[...], axis=0, keepdims=True))
+        score = jnp.sum(part * score_left[...], axis=0, keepdims=True)
         cos, sin = phase[shift, 0], phase[shift, 1]
         con_re, con_im = re * cos - im * sin, im * cos + re * sin
         tail = jnp.where((tail_row == 1) & (lane == bin_at), live, con_re[side // 2 :])
-        total[local, : side // 2] += con_re[: side // 2]
-        total[local, side // 2 : HALF] += tail
-        total[local, HALF:] += con_im
-    found = jnp.concatenate(rows, axis=0)
-    scores[0] = found + pltpu.roll(found, found.shape[1] // 2, 1)
-
-
-def owner_terms(images, info, start, refs, tables):
-    sources, held, side = images.shape
-    per_source = held // side
-    count = sources * per_source
-    block = math.gcd(sources, max(1, GROUP // per_source))
-    group = block * per_source
+        return score, jnp.concatenate([con_re[: side // 2], tail, con_im], axis=0)
+
+    def chunk(r, carry):
+        for d in range(1, owners):
+            copy(r, d).wait()
+
+        @pl.when(r + 2 < chunks)
+        def _():
+            for d in range(1, owners):
+                copy(r + 2, d).start()
+
+        def sources(step, inner):
+            base = (r * owners + step * block) * slots
+            found, parts = [], []
+            for n in range(block * slots):
+                start = pl.multiple_of(r * span + n % slots * side, side)
+                score, part = particle(
+                    base + n, got[step * block + n // slots, pl.ds(start, side)]
+                )
+                found.append(score)
+                parts.append(part)
+            for n in range(block * slots):
+                running[base + n + 1] = running[info[5, base + n]] + parts[n]
+            found = jnp.concatenate(found, axis=0)
+            found = found + pltpu.roll(found, found.shape[1] // 2, 1)
+            for n in range(block):
+                scores[r, step * block + n] = found[n * slots : (n + 1) * slots]
+            return inner
+
+        return lax.fori_loop(0, owners // block, sources, carry)
+
+    lax.fori_loop(0, chunks, chunk, 0)
+
+    def close_class(c, carry):
+        total[c] = running[last[c]]
+        return carry
+
+    lax.fori_loop(0, classes, close_class, 0)
+
+
+def gather_terms(send, info, last, references, tables, chunks):
+    owners, held, side = send.shape
+    slots = held // side // chunks
+    class_local = references.shape[0]
     contrast, phase, right, left, score_right, score_left = tables
-    whole = lambda x: pl.BlockSpec(
-        x.shape, lambda i, info: (0,) * x.ndim, pipeline_mode=pl.Buffered(1)
-    )
-    fixed = (refs, contrast, phase, *right, *left, *score_right, score_left, start)
     lanes = score_left.shape[1]
+    vmem = pl.BlockSpec(memory_space=pltpu.VMEM)
+    smem = pl.BlockSpec(memory_space=pltpu.SMEM)
+    hbm = pl.BlockSpec(memory_space=pl.ANY)
+    dma = pltpu.SemaphoreType.DMA
     return pl.pallas_call(
-        functools.partial(owner_kernel, side),
-        grid_spec=pltpu.PrefetchScalarGridSpec(
-            num_scalar_prefetch=1,
-            grid=(sources // block,),
-            in_specs=[pl.BlockSpec((block, held, side), lambda i, info: (i, 0, 0))]
-            + [whole(x) for x in fixed],
-            out_specs=[
-                pl.BlockSpec((1, group, lanes), lambda i, info: (i, 0, 0)),
-                pl.BlockSpec(start.shape, lambda i, info: (0, 0, 0)),
-            ],
+        functools.partial(gather_kernel, side, owners, chunks),
+        in_specs=[smem, smem, hbm, hbm, hbm] + [vmem] * 8,
+        out_specs=[vmem, vmem],
+        out_shape=[
+            jax.ShapeDtypeStruct((chunks, owners, slots, lanes), f32),
+            jax.ShapeDtypeStruct((class_local, 2 * HALF, side), f32),
+        ],
+        scratch_shapes=[
+            pltpu.VMEM(send.shape, f32),
+            pltpu.VMEM(references.shape, f32),
+            pltpu.VMEM(phase.shape, f32),
+            pltpu.VMEM((class_local, 2, HALF, side), f32),
+            pltpu.VMEM((owners * slots * chunks + 1, 2 * HALF, side), f32),
+            dma((chunks, owners)),
+            dma((chunks, owners)),
+            dma((3,)),
+        ],
+        compiler_params=pltpu.CompilerParams(
+            collective_id=1, has_side_effects=True, vmem_limit_bytes=VMEM_BYTES
         ),
-        out_shape=[
-            jax.ShapeDtypeStruct((sources // block, group, lanes), f32),
-            jax.ShapeDtypeStruct(start.shape, f32),
-        ],
-        compiler_params=pltpu.CompilerParams(vmem_limit_bytes=VMEM_BYTES),
         cost_estimate=pl.CostEstimate(
-            flops=count * 70_000_000, bytes_accessed=count * side * side * 4 + 14_000_000,
+            flops=owners * slots * chunks * 70_000_000, bytes_accessed=30_000_000,
             transcendentals=0,
         ),
-        name="owner_terms",
-    )(info, images, *fixed)
+        name="gather_terms",
+    )(info, last, send, references, phase, contrast, *right, *left, *score_right, score_left)
 
 
 def finish_class(side, bins, share, contrast, out, n):
@@ -347,65 +397,44 @@
     shifts = shift_list.shape[0]
     owners = lax.axis_size("cls")
     capacity = max(2, 2 * part_rows // owners)
-    last = max(1, capacity // 4)
-    chunks = (capacity - last, last)
-    starts = (0, owners * chunks[0])
+    chunks = math.gcd(capacity, 4)
+    slots = capacity // chunks
     slot_total = owners * capacity
 
-    def places(classes):
-        owner = classes // class_local
-        rows = jnp.arange(part_rows)
-        before = rows[:, None] > rows[None, :]
-        same = owner[..., :, None] == owner[..., None, :]
-        return owner, jnp.sum((before & same).astype(jnp.int32), axis=-1)
-
-    owner_of, rank = places(class_of)
-    target = jnp.where(
-        rank < chunks[0],
-        owner_of * chunks[0] + rank,
-        starts[1] + owner_of * chunks[1] + rank - chunks[0],
-    )
+    owner_of = class_of // class_local
+    rows = jnp.arange(part_rows)
+    before = (rows[:, None] > rows[None, :]) & (owner_of[:, None] == owner_of[None, :])
+    rank = jnp.sum(before.astype(jnp.int32), axis=1)
+    target = owner_of * capacity + rank
     hit = target[None, :] == jnp.arange(slot_total, dtype=jnp.int32)[:, None]
-    source = jnp.sum(jnp.where(hit, jnp.arange(part_rows, dtype=jnp.int32)[None, :], 0), axis=1)
-    send = [
-        particles[source[s : s + owners * c]].reshape(owners, c * side, side)
-        for s, c in zip(starts, chunks)
-    ]
     facts = jnp.stack(
         [class_of % class_local, defocus_bin, shift_best, rotation_bin, jnp.ones_like(class_of)]
     )
-    place = (owner_of * capacity + rank)[None, :] == jnp.arange(slot_total, dtype=jnp.int32)[:, None]
-    facts = jnp.sum(jnp.where(place[None], facts[:, None, :], 0), axis=2).astype(f32)
+    facts = jnp.sum(jnp.where(hit[None], facts[:, None, :], 0), axis=2).astype(f32)
     facts = facts.reshape(5, owners, capacity).transpose(1, 0, 2)
-    facts = jnp.pad(facts, ((0, 0), (0, 3), (0, side - capacity)))
-    send[0] = jnp.concatenate([send[0], facts], axis=1)
-
-    exchange = lambda x: lax.all_to_all(x, "cls", split_axis=0, concat_axis=0, tiled=True)
+    facts = lax.all_to_all(facts, "cls", split_axis=0, concat_axis=0, tiled=True)
+    source = jnp.sum(jnp.where(hit, rows.astype(jnp.int32)[None, :], 0), axis=1)
+    send = particles[source].reshape(owners, capacity * side, side)
+
     right, left = dft_tables(side)
     contrast = contrast_half(defocus, side)
     phase, score_right, score_left = shift_tables(shift_list, side)
     tables = (contrast, phase, split_table(right), split_table(left), split_table(score_right), score_left)
-    refs = reference_half(references)
-    got = [exchange(send[0])]
-    got[0], send[1], refs, tables = lax.optimization_barrier((got[0], send[1], refs, tables))
-    got.append(exchange(send[1]))
-
-    facts = got[0][:, chunks[0] * side : chunks[0] * side + 5, :capacity].astype(jnp.int32)
-    facts = facts.transpose(1, 0, 2)
-    info = [
-        facts[:, :, : chunks[0]].reshape(5, -1),
-        facts[:, :, chunks[0] :].reshape(5, -1),
-    ]
-
-    total = jnp.zeros((class_local, 2 * HALF, side), f32)
-    found = []
-    for h in (0, 1):
-        scores, total = owner_terms(got[h], info[h], total, refs, tables)
-        found.append(scores.reshape(owners, chunks[h], -1))
-    found = jnp.concatenate(found, axis=1)
+
+    facts = facts.astype(jnp.int32).reshape(owners, 5, chunks, slots).transpose(1, 2, 0, 3)
+    facts = facts.reshape(5, slot_total)
+    count = jnp.arange(slot_total, dtype=jnp.int32)
+    alike = (facts[0][:, None] == facts[0][None, :]) & (facts[4][None, :] > 0)
+    alike = alike & (count[None, :] < count[:, None])
+    earlier = jnp.max(jnp.where(alike, count[None, :] + 1, 0), axis=1)
+    of_class = facts[0][None, :] == jnp.arange(class_local, dtype=jnp.int32)[:, None]
+    last = jnp.max(jnp.where(of_class & (facts[4][None, :] > 0), count[None, :] + 1, 0), axis=1)
+    info = jnp.concatenate([facts, earlier[None]], axis=0)
+
+    found, total = gather_terms(send, info, last, references, tables, chunks)
+    found = found.transpose(1, 0, 2, 3).reshape(owners, capacity, -1)
     fresh, home = close(total, found, contrast, lax.axis_size("grp"), owners)
-    home = home.reshape(slot_total, -1)
-    return home[owner_of * capacity + rank][:, :shifts], fresh
+    return home.reshape(slot_total, -1)[target][:, :shifts], fresh
 
 
 def solution(mesh):

time: 165 us -> 163 us (0.988)
  Pallas kernels: 72.6 us -> 129 us
  waiting for transfers between devices: 48 us -> 0.01 us
  other arithmetic: 19 us -> 14.4 us
  starting transfers between devices: 10.9 us -> 7.25 us
  local copies, waits for them, and re-layouts: 13.1 us -> 11.3 us
    pallas_call x3 -> x1, Pallas kernels: 47.2 us -> 96.8 us  [gather_terms(): pl.pallas_call(functools.partial(gather_kernel, side, owners, chunks), in...]
    all_to_all x2 -> x1, waiting for transfers between devices: 48 us -> 0.01 us  [body(): lax.all_to_all(facts, 'cls', split_axis=0, concat_axis=0, tiled=True)]
    pallas_call x1, Pallas kernels: 25.4 us -> 32 us  [close(): pl.pallas_call(functools.partial(close_kernel, side, contrast.shape[0], g...]
    concatenate x2 -> x1, other arithmetic: 5.18 us -> 0.61 us  [body(): info = jnp.concatenate([facts, earlier[None]], axis=0)]
    all_to_all x2 -> x1, starting transfers between devices: 10.9 us -> 7.25 us  [body(): lax.all_to_all(facts, 'cls', split_axis=0, concat_axis=0, tiled=True)]
    transpose x0 -> x3, local copies, waits for them, and re-layouts: none -> 2.12 us  [the longest x1 1.37 us: body(): found = found.transpose(1, 0, 2, 3).reshape(owners, capacity, -1)]
    gather x3 -> x2, local copies, waits for them, and re-layouts: 5.91 us -> 4.76 us  [the longest x1 2.84 us: body(): send = particles[source].reshape(owners, capacity * side, side)]
  transfers between devices with their start and end apart: 2 -> 1, of which waited for: 1 -> 0; matrix products, arithmetic and copies ran while one was open for 10% -> 9% of each run, Pallas kernels for 21% -> 0%
where the time goes in v3:
time: 163 us
  Pallas kernels  129 us (79%)
  other arithmetic  14.4 us (9%)
  local copies, waits for them, and re-layouts  11.3 us (7%)
  starting transfers between devices  7.25 us (4%)
    pallas_call x1, Pallas kernels, gather_terms(): pl.pallas_call(functools.partial(gather_kernel, side, owners, chunks), in...  96.8 us
    pallas_call x1, Pallas kernels, close(): pl.pallas_call(functools.partial(close_kernel, side, contrast.shape[0], g...  32 us
    all_to_all x1, starting transfers between devices, body(): lax.all_to_all(facts, 'cls', split_axis=0, concat_axis=0, tiled=True)  7.25 us
  transfers between devices with their start and end apart: 1, of which 0 were waited for; matrix products, arithmetic and copies ran while one was open for 9% of the time, Pallas kernels for 0%

profile of v3, /device:TPU:0, one launch (start us, length us, event | category | flops | bytes accessed | tf_op | source)
XLA Modules:
  0.0 162.7 jit_solution(14683857119909761594)
XLA Ops:
  0.6 0.8 and_select_fusion.1
  1.5 0.2 convert_reduce_fusion
  1.7 0.7 stack.42
  2.6 0.6 copy.36
  3.2 7.3 %all-to-all-start = ((f32[8,5,8]{2,1,0:T(8,128)}), f32[8,5,8]{2,1,0:T(8,128)S(1)}, u32[]{:S(2)}, u32[]{:S(2)}) async-start(f32[8,5,8]{2,1,0:T(8,128)} %copy.36), calls=%async_computation | async-start | bytes 65536 | tf_op jit(solution)/shard_map/all_to_all | solution.py:415
  10.5 0.3 sine_multiply_fusion.1
  10.8 0.8 slice_bitcast_fusion.1
  11.6 0.2 fusion.57
  11.8 0.3 fusion.48
  12.2 0.4 fusion.18
  12.5 0.2 fusion.59
  12.8 0.2 cosine_multiply_fusion.2
  13.0 0.2 fusion.68
  13.2 0.8 fusion.5
  14.0 1.3 multiply_subtract_fusion
  15.3 2.4 %pad_maximum_fusion.phase_in = f32[64,2,72,128]{3,2,1,0:T(8,128)} fusion(f32[64,1,72,128]{3,2,1,0:T(8,128)S(1)} %get-tuple-element.23, f32[64,1,72,128]{3,2,1,0:T(8,128)S(1)} %get-tuple-element.22), kind=kLoop, calls=%fused_computation.2 | loop fusion | flops 1179648 | bytes 9437184 | tf_op jit(solution)/shard_map/stack | solution.py:84
  17.7 0.8 fusion.7
  18.5 0.7 fusion.9
  19.3 3.2 %fusion.2.contrast = f32[16,72,128]{2,1,0:T(8,128)} fusion(f32[72,128]{1,0:T(8,128)S(1)} %add_multiply_fusion, f32[16]{0:T(128)S(1)} %copy-done.1), kind=kLoop, calls=%fused_computation.9 | loop fusion | flops 737280 | bytes 626752 | tf_op jit(solution)/shard_map/neg | solution.py:72
  22.5 0.7 maximum_maximum_fusion.score_left
  23.2 2.8 %gather_fusion = f32[64,128,128]{2,1,0:T(8,128)} fusion(f32[32,128,128]{2,1,0:T(8,128)S(1)} %copy-done, s32[1024]{0:T(1024)S(1)} %pad_clamp_fusion.1), kind=kCustom, calls=%fused_computation | custom fusion | bytes 8388864 | tf_op jit(solution)/shard_map/gather | solution.py:417
  26.2 0.1 copy.39
  26.5 0.1 copy.41
  26.6 0.1 gt.29
  26.7 0.2 select_reduce_fusion.1
  26.9 0.7 select_reduce_fusion.3.last
  27.6 0.6 pad_add_fusion.info
  28.3 96.8 %gather_terms.1 = (f32[4,8,2,128]{3,2,1,0:T(2,128)}, f32[32,144,128]{2,1,0:T(8,128)}) custom-call(s32[6,64]{1,0:T(8,128)} %pad_add_fusion.info, s32[32]{0:T(128)} %select_reduce_fusion.3.last, f32[8,1024,128]{2,1,0:T(8,128)} %bitcast.38, f32[32,2,128,128]{3,2,1,0:T(8,128)} %references.1, f32[64,2,72,128]{3,2,1,0:T(8,128)} %pad_maximum_fusion.phase_in, ...), custom_call_target="tpu_custom_call" | custom-call | flops 4480000000 | bytes 30000000 | tf_op jit(solution)/shard_map/gather_terms/pallas_call | solution.py:239
  125.1 1.4 copy.43
  126.4 32.0 %close.1 = (f32[8,2,128,128]{3,2,1,0:T(8,128)}, f32[8,8,128]{2,1,0:T(8,128)}) custom-call(f32[2,2,8,144,128]{4,3,2,1,0:T(8,128)} %bitcast.39, f32[8,8,128]{2,1,0:T(8,128)} %bitcast.41, f32[16,72,128]{2,1,0:T(8,128)} %fusion.2.contrast), custom_call_target="tpu_custom_call" | custom-call | flops 160000000 | bytes 8000000 | tf_op jit(solution)/shard_map/close/pallas_call | solution.py:361
  158.5 1.9 %gather_fusion.1 = f32[32,128]{1,0:T(8,128)} fusion(f32[64,128]{1,0:T(8,128)} %bitcast.40, s32[1024]{0:T(1024)S(1)} %pad_clamp_fusion), kind=kCustom, calls=%fused_computation.1 | custom fusion | bytes 32896 | tf_op jit(solution)/shard_map/gather | solution.py:437
  160.4 2.3 %copy.47 = f32[8,2,128,128]{3,2,1,0:T(8,128)} copy(f32[8,2,128,128]{3,2,1,0:T(8,128)} %get-tuple-element.51) | data formatting | bytes 2097152
  (35 shorter events, 0.9 us)
Async XLA Ops:
  0.6 22.6 %copy-start = (f32[32,128,128]{2,1,0:T(8,128)S(1)}, f32[32,128,128]{2,1,0:T(8,128)}, u32[]{:S(2)}) copy-start(f32[32,128,128]{2,1,0:T(8,128)} %param.8) | copy-start | bytes 6291460
  3.2 22.8 %all-to-all-start = ((f32[8,5,8]{2,1,0:T(8,128)}), f32[8,5,8]{2,1,0:T(8,128)S(1)}, u32[]{:S(2)}, u32[]{:S(2)}) async-start(f32[8,5,8]{2,1,0:T(8,128)} %copy.36), calls=%async_computation | async-start | bytes 65536 | tf_op jit(solution)/shard_map/all_to_all | solution.py:415
  15.2 4.0 %copy-start.1 = (f32[16]{0:T(128)S(1)}, f32[16]{0:T(128)}, u32[]{:S(2)}) copy-start(f32[16]{0:T(128)} %param.15) | copy-start | bytes 196

commit v4 on v3

--- a/solution.py
+++ b/solution.py
@@ -3,6 +3,8 @@
 
 import jax
 import jax.numpy as jnp
+import ml_dtypes
+import numpy as np
 from jax import lax
 from jax.experimental import pallas as pl
 from jax.experimental.pallas import tpu as pltpu
@@ -11,6 +13,7 @@
 f32, bf16 = jnp.float32, jnp.bfloat16
 HALF = 72
 GROUP = 8
+AHEAD = 3
 VMEM_BYTES = 56 * 1024 * 1024
 
 
@@ -38,27 +41,23 @@
 
 
 def dft_tables(side):
-    pixel = jnp.arange(side, dtype=jnp.int32)
-    norm = 1.0 / math.sqrt(side)
-    cos_table, sin_table = circle(pixel[:, None] * pixel[None, :], side)
-    cos_table, sin_table = cos_table * norm, sin_table * norm
-    flip_cos, flip_sin = circle(pixel[:, None] * (side - 1 - pixel)[None, :], side)
-    flip_cos, flip_sin = flip_cos * norm, flip_sin * norm
-    right = jnp.stack(
-        [
-            jnp.concatenate([cos_table, sin_table], axis=1),
-            jnp.concatenate([flip_cos.T, flip_sin.T], axis=1),
-        ]
-    )
-    live = (jnp.arange(HALF) <= side // 2)[:, None].astype(f32)
-
-    def left(c, s):
+    pixel = np.arange(side)
+    live = (np.arange(HALF) <= side // 2)[:, None]
+    right, left = [], []
+    for place in (pixel, side - 1 - pixel):
+        angles = (pixel[:, None] * place[None, :] % side) * (2.0 * math.pi / side)
+        c, s = np.cos(angles) / math.sqrt(side), np.sin(angles) / math.sqrt(side)
+        right.append(np.concatenate([c.T, s.T], axis=1))
         c, s = c[:HALF] * live, s[:HALF] * live
-        return jnp.concatenate(
-            [jnp.concatenate([c, -s], axis=1), jnp.concatenate([-s, -c], axis=1)], axis=0
-        )
-
-    return right, jnp.stack([left(cos_table, sin_table), left(flip_cos, flip_sin)])
+        left.append(np.block([[c, -s], [-s, -c]]))
+
+    def halves(x):
+        x = np.stack(x)
+        high = x.astype(ml_dtypes.bfloat16)
+        low = (x - high.astype(np.float64)).astype(ml_dtypes.bfloat16)
+        return jnp.asarray(high), jnp.asarray(low)
+
+    return halves(right), halves(left)
 
 
 def contrast_half(defocus, side):
@@ -79,9 +78,8 @@
     col_cos, col_sin = circle(
         shift_list[:, 1][:, None] * jnp.arange(side, dtype=jnp.int32)[None, :], side
     )
-    rc, rs = row_cos[:, :, None], row_sin[:, :, None]
-    cc, cs = col_cos[:, None, :], col_sin[:, None, :]
-    phase = jnp.stack([rc * cc - rs * cs, rs * cc + rc * cs], axis=1)
+    row_table = jnp.concatenate([row_cos.T, row_sin.T], axis=0)
+    col_table = jnp.stack([col_cos, col_sin], axis=1)
     score_right = jnp.concatenate([col_cos.T, col_sin.T], axis=1)
     row = jnp.arange(HALF)
     times = jnp.where(
@@ -91,7 +89,7 @@
     score_left = jnp.concatenate(
         [jnp.concatenate([uc, -us], axis=1), jnp.concatenate([-us, -uc], axis=1)], axis=0
     )
-    return phase, score_right, score_left
+    return row_table, col_table, score_right, score_left
 
 
 def mirror_pick(rows, cols, side, offset):
@@ -109,9 +107,10 @@
 
 
 def gather_kernel(
-    side, owners, chunks, info, last, send, references, phase_in, contrast,
+    side, owners, chunks, facts, send, references, contrast, row_table, col_table,
     right_hi, right_lo, left_hi, left_lo, sr_hi, sr_lo, score_left, scores, total,
-    got, held_refs, phase, refs, running, send_sem, recv_sem, local_sem,
+    got, held_refs, refs, running, fact_board, info, newest, last, earlier,
+    send_sem, recv_sem, fact_send, fact_recv, local_sem,
 ):
     mesh_ids = pl.DeviceIdType.MESH
     cls = lax.axis_index("cls")
@@ -121,8 +120,7 @@
 
     local_copies = [
         pltpu.make_async_copy(references, held_refs, local_sem.at[0]),
-        pltpu.make_async_copy(phase_in, phase, local_sem.at[1]),
-        pltpu.make_async_copy(send.at[cls], got.at[cls], local_sem.at[2]),
+        pltpu.make_async_copy(send.at[cls], got.at[cls], local_sem.at[1]),
     ]
 
     def copy(r, d):
@@ -142,7 +140,17 @@
     for made in local_copies:
         made.start()
     pl.semaphore_wait(barrier, owners - 1)
-    for r in range(min(2, chunks)):
+    fact_copies = []
+    for d in range(1, owners):
+        to = lax.rem(cls + d, owners)
+        made = pltpu.make_async_remote_copy(
+            src_ref=facts.at[to], dst_ref=fact_board.at[cls],
+            send_sem=fact_send.at[d], recv_sem=fact_recv.at[d],
+            device_id={"cls": to}, device_id_type=mesh_ids,
+        )
+        made.start()
+        fact_copies.append(made)
+    for r in range(min(AHEAD, chunks)):
         for d in range(1, owners):
             copy(r, d).start()
 
@@ -164,13 +172,37 @@
 
     lax.fori_loop(0, classes // at_once, halve, 0)
 
+    fact_board[cls] = facts[cls]
+    for made in fact_copies:
+        made.wait()
+    to_scalars = pltpu.make_async_copy(fact_board, info, local_sem.at[2])
+    to_scalars.start()
+    to_scalars.wait()
+    lanes = lax.broadcasted_iota(jnp.int32, (8, side), 1)
+
+    def chain(n, seen):
+        source, at = n // slots % owners, n // (slots * owners) * slots + n % slots
+        key = info[source, 0, at] + (1 - info[source, 4, at]) * classes
+        mine = lanes == key
+        earlier[n] = jnp.max(jnp.where(mine, seen, 0))
+        return jnp.where(mine, n + 1, seen)
+
+    newest[...] = lax.fori_loop(
+        0, owners * slots * chunks, chain, jnp.zeros((8, side), jnp.int32)
+    )
+    to_scalars = pltpu.make_async_copy(newest, last, local_sem.at[3])
+    to_scalars.start()
+    to_scalars.wait()
+
     lane = lax.broadcasted_iota(jnp.int32, (8, side), 1)
     tail_row = lax.broadcasted_iota(jnp.int32, (8, side), 0)
     block = math.gcd(owners, max(1, GROUP // slots))
 
-    def particle(at, image):
-        bin_at, shift = info[1, at], info[2, at]
-        local, turns, live = info[0, at], info[3, at], info[4, at].astype(f32)
+    shift_lane = lax.broadcasted_iota(jnp.int32, row_table.shape, 1)
+
+    def particle(source, at, image):
+        local, bin_at, shift = info[source, 0, at], info[source, 1, at], info[source, 2, at]
+        turns, live = info[source, 3, at], info[source, 4, at].astype(f32)
         image = jnp.where(turns % 2 == 1, image.T, image)
         right_at = (turns >= 2).astype(jnp.int32)
         left_at = ((turns == 1) | (turns == 2)).astype(jnp.int32)
@@ -183,7 +215,10 @@
         product = jnp.concatenate([re * ref_re + im * ref_im, im * ref_re - re * ref_im], axis=0)
         part = dot3(split(product), (sr_hi[...], sr_lo[...]))
         score = jnp.sum(part * score_left[...], axis=0, keepdims=True)
-        cos, sin = phase[shift, 0], phase[shift, 1]
+        factor = jnp.sum(jnp.where(shift_lane == shift, row_table[...], 0.0), axis=1, keepdims=True)
+        col = col_table[shift]
+        cos = factor[:HALF] * col[:1] - factor[HALF:] * col[1:]
+        sin = factor[HALF:] * col[:1] + factor[:HALF] * col[1:]
         con_re, con_im = re * cos - im * sin, im * cos + re * sin
         tail = jnp.where((tail_row == 1) & (lane == bin_at), live, con_re[side // 2 :])
         return score, jnp.concatenate([con_re[: side // 2], tail, con_im], axis=0)
@@ -192,10 +227,10 @@
         for d in range(1, owners):
             copy(r, d).wait()
 
-        @pl.when(r + 2 < chunks)
+        @pl.when(r + AHEAD < chunks)
         def _():
             for d in range(1, owners):
-                copy(r + 2, d).start()
+                copy(r + AHEAD, d).start()
 
         def sources(step, inner):
             base = (r * owners + step * block) * slots
@@ -203,12 +238,13 @@
             for n in range(block * slots):
                 start = pl.multiple_of(r * span + n % slots * side, side)
                 score, part = particle(
-                    base + n, got[step * block + n // slots, pl.ds(start, side)]
+                    step * block + n // slots, r * slots + n % slots,
+                    got[step * block + n // slots, pl.ds(start, side)],
                 )
                 found.append(score)
                 parts.append(part)
             for n in range(block * slots):
-                running[base + n + 1] = running[info[5, base + n]] + parts[n]
+                running[base + n + 1] = running[earlier[base + n]] + parts[n]
             found = jnp.concatenate(found, axis=0)
             found = found + pltpu.roll(found, found.shape[1] // 2, 1)
             for n in range(block):
@@ -220,25 +256,24 @@
     lax.fori_loop(0, chunks, chunk, 0)
 
     def close_class(c, carry):
-        total[c] = running[last[c]]
+        total[c] = running[last[0, c]]
         return carry
 
     lax.fori_loop(0, classes, close_class, 0)
 
 
-def gather_terms(send, info, last, references, tables, chunks):
+def gather_terms(send, facts, references, tables, chunks):
     owners, held, side = send.shape
     slots = held // side // chunks
     class_local = references.shape[0]
-    contrast, phase, right, left, score_right, score_left = tables
+    contrast, row_table, col_table, right, left, score_right, score_left = tables
     lanes = score_left.shape[1]
     vmem = pl.BlockSpec(memory_space=pltpu.VMEM)
-    smem = pl.BlockSpec(memory_space=pltpu.SMEM)
     hbm = pl.BlockSpec(memory_space=pl.ANY)
     dma = pltpu.SemaphoreType.DMA
     return pl.pallas_call(
         functools.partial(gather_kernel, side, owners, chunks),
-        in_specs=[smem, smem, hbm, hbm, hbm] + [vmem] * 8,
+        in_specs=[vmem, hbm, hbm] + [vmem] * 10,
         out_specs=[vmem, vmem],
         out_shape=[
             jax.ShapeDtypeStruct((chunks, owners, slots, lanes), f32),
@@ -247,12 +282,18 @@
         scratch_shapes=[
             pltpu.VMEM(send.shape, f32),
             pltpu.VMEM(references.shape, f32),
-            pltpu.VMEM(phase.shape, f32),
             pltpu.VMEM((class_local, 2, HALF, side), f32),
             pltpu.VMEM((owners * slots * chunks + 1, 2 * HALF, side), f32),
+            pltpu.VMEM(facts.shape, jnp.int32),
+            pltpu.SMEM(facts.shape, jnp.int32),
+            pltpu.VMEM((8, side), jnp.int32),
+            pltpu.SMEM((8, side), jnp.int32),
+            pltpu.SMEM((owners * slots * chunks,), jnp.int32),
             dma((chunks, owners)),
             dma((chunks, owners)),
-            dma((3,)),
+            dma((owners,)),
+            dma((owners,)),
+            dma((4,)),
         ],
         compiler_params=pltpu.CompilerParams(
             collective_id=1, has_side_effects=True, vmem_limit_bytes=VMEM_BYTES
@@ -262,7 +303,9 @@
             transcendentals=0,
         ),
         name="gather_terms",
-    )(info, last, send, references, phase, contrast, *right, *left, *score_right, score_left)
+    )(
+        facts, send, references, contrast, row_table, col_table, *right, *left, *score_right, score_left
+    )
 
 
 def finish_class(side, bins, share, contrast, out, n):
@@ -397,7 +440,7 @@
     shifts = shift_list.shape[0]
     owners = lax.axis_size("cls")
     capacity = max(2, 2 * part_rows // owners)
-    chunks = math.gcd(capacity, 4)
+    chunks = math.gcd(capacity, 8)
     slots = capacity // chunks
     slot_total = owners * capacity
 
@@ -410,28 +453,18 @@
     facts = jnp.stack(
         [class_of % class_local, defocus_bin, shift_best, rotation_bin, jnp.ones_like(class_of)]
     )
-    facts = jnp.sum(jnp.where(hit[None], facts[:, None, :], 0), axis=2).astype(f32)
+    facts = jnp.sum(jnp.where(hit[None], facts[:, None, :], 0), axis=2)
     facts = facts.reshape(5, owners, capacity).transpose(1, 0, 2)
-    facts = lax.all_to_all(facts, "cls", split_axis=0, concat_axis=0, tiled=True)
+    facts = jnp.pad(facts, ((0, 0), (0, 3), (0, side - capacity)))
     source = jnp.sum(jnp.where(hit, rows.astype(jnp.int32)[None, :], 0), axis=1)
     send = particles[source].reshape(owners, capacity * side, side)
 
     right, left = dft_tables(side)
     contrast = contrast_half(defocus, side)
-    phase, score_right, score_left = shift_tables(shift_list, side)
-    tables = (contrast, phase, split_table(right), split_table(left), split_table(score_right), score_left)
-
-    facts = facts.astype(jnp.int32).reshape(owners, 5, chunks, slots).transpose(1, 2, 0, 3)
-    facts = facts.reshape(5, slot_total)
-    count = jnp.arange(slot_total, dtype=jnp.int32)
-    alike = (facts[0][:, None] == facts[0][None, :]) & (facts[4][None, :] > 0)
-    alike = alike & (count[None, :] < count[:, None])
-    earlier = jnp.max(jnp.where(alike, count[None, :] + 1, 0), axis=1)
-    of_class = facts[0][None, :] == jnp.arange(class_local, dtype=jnp.int32)[:, None]
-    last = jnp.max(jnp.where(of_class & (facts[4][None, :] > 0), count[None, :] + 1, 0), axis=1)
-    info = jnp.concatenate([facts, earlier[None]], axis=0)
-
-    found, total = gather_terms(send, info, last, references, tables, chunks)
+    row_table, col_table, score_right, score_left = shift_tables(shift_list, side)
+    tables = (contrast, row_table, col_table, right, left, split_table(score_right), score_left)
+
+    found, total = gather_terms(send, facts, references, tables, chunks)
     found = found.transpose(1, 0, 2, 3).reshape(owners, capacity, -1)
     fresh, home = close(total, found, contrast, lax.axis_size("grp"), owners)
     return home.reshape(slot_total, -1)[target][:, :shifts], fresh

time: 163 us -> 149 us (0.914)
  starting transfers between devices: 7.25 us -> 0 us
  other arithmetic: 14.4 us -> 8.73 us
    all_to_all x1 -> x0, starting transfers between devices: 7.25 us -> none  [body(): lax.all_to_all(facts, 'cls', split_axis=0, concat_axis=0, tiled=True)]
    pallas_call x1, Pallas kernels: 96.8 us -> 101 us  [gather_terms(): pl.pallas_call(functools.partial(gather_kernel, side, owners, chunks), in...]
    pallas_call x1, Pallas kernels: 32 us -> 27.7 us  [close(): pl.pallas_call(functools.partial(close_kernel, side, contrast.shape[0], g...]
    transpose x3 -> x0, local copies, waits for them, and re-layouts: 2.12 us -> none  [the longest x1 1.37 us: body(): found = found.transpose(1, 0, 2, 3).reshape(owners, capacity, -1)]
    another operation x5 -> x1, other arithmetic: 2.48 us -> 0.7 us  [shift_tables(): col_table = jnp.stack([col_cos, col_sin], axis=1)]
  transfers between devices with their start and end apart: 1 -> 0, of which waited for: 0 -> 0; matrix products, arithmetic and copies ran while one was open for 9% -> 0% of each run, Pallas kernels for 0% -> 0%
where the time goes in v4:
time: 149 us
  Pallas kernels  129 us (87%)
  local copies, waits for them, and re-layouts  10.6 us (7%)
  other arithmetic  8.73 us (6%)
    pallas_call x1, Pallas kernels, gather_terms(): pl.pallas_call(functools.partial(gather_kernel, side, owners, chunks), in...  101 us
    pallas_call x1, Pallas kernels, close(): pl.pallas_call(functools.partial(close_kernel, side, contrast.shape[0], g...  27.7 us
    neg x1, other arithmetic, contrast_half(): return -(0.995 * jnp.sin(phases) + 0.1 * jnp.cos(phases))  3.19 us

profile of v4, /device:TPU:0, one launch (start us, length us, event | category | flops | bytes accessed | tf_op | source)
XLA Modules:
  0.0 148.9 jit_solution(13375969727749274111)
XLA Ops:
  0.6 0.0 copy-start
  0.6 0.8 slice_bitcast_fusion
  1.5 0.2 broadcast_multiply_fusion
  1.7 0.7 maximum_maximum_fusion.score_left
  2.4 0.6 pad_maximum_fusion.row_table
  3.0 0.3 fusion.21
  3.3 0.7 fusion.5
  4.0 0.7 and_select_fusion.1
  4.7 0.2 convert_reduce_fusion
  4.9 0.1 iota_compare_fusion
  5.0 0.7 stack.24
  5.7 0.1 select_reduce_fusion
  5.8 0.1 reshape.214
  5.9 0.6 pad.4.facts
  6.5 0.1 select_reduce_fusion.1
  6.6 0.0 copy-done
  6.6 0.0 copy-start.1
  6.6 2.7 %gather_fusion = f32[64,128,128]{2,1,0:T(8,128)} fusion(f32[32,128,128]{2,1,0:T(8,128)S(1)} %copy-done, s32[1024]{0:T(1024)S(1)} %pad_clamp_fusion.1), kind=kCustom, calls=%fused_computation | custom fusion | bytes 8388864 | tf_op jit(solution)/shard_map/gather | solution.py:460
  9.4 0.1 fusion.19
  9.5 1.0 multiply_cosine_fusion.1
  10.5 0.7 pad_maximum_fusion.1.col_table
  11.2 0.1 add_multiply_fusion
  11.3 0.0 copy-done.1
  11.3 3.2 %fusion.2.contrast = f32[16,72,128]{2,1,0:T(8,128)} fusion(f32[72,128]{1,0:T(8,128)S(1)} %add_multiply_fusion, f32[16]{0:T(128)S(1)} %copy-done.1), kind=kLoop, calls=%fused_computation.6 | loop fusion | flops 737280 | bytes 626752 | tf_op jit(solution)/shard_map/neg | solution.py:71
  14.5 101.2 %gather_terms.1 = (f32[8,8,1,128]{3,2,1,0:T(1,128)}, f32[32,144,128]{2,1,0:T(8,128)}) custom-call(s32[8,8,128]{2,1,0:T(8,128)} %pad.4.facts, f32[8,1024,128]{2,1,0:T(8,128)} %bitcast.26, f32[32,2,128,128]{3,2,1,0:T(8,128)} %references.1, f32[16,72,128]{2,1,0:T(8,128)} %fusion.2.contrast, f32[144,64]{1,0:T(8,128)} %pad_maximum_fusion.row_table, ...), custom_call_target="tpu_custom_call" | custom-call | flops 4480000000 | bytes 30000000 | tf_op jit(solution)/shard_map/gather_terms/pallas_call | solution.py:274
  115.7 1.4 copy.24
  117.0 27.7 %close.1 = (f32[8,2,128,128]{3,2,1,0:T(8,128)}, f32[8,8,128]{2,1,0:T(8,128)}) custom-call(f32[2,2,8,144,128]{4,3,2,1,0:T(8,128)} %bitcast.27, f32[8,8,128]{2,1,0:T(8,128)} %bitcast.29, f32[16,72,128]{2,1,0:T(8,128)} %fusion.2.contrast), custom_call_target="tpu_custom_call" | custom-call | flops 160000000 | bytes 8000000 | tf_op jit(solution)/shard_map/close/pallas_call | solution.py:404
  144.7 1.9 %gather_fusion.1 = f32[32,128]{1,0:T(8,128)} fusion(f32[64,128]{1,0:T(8,128)} %bitcast.28, s32[1024]{0:T(1024)S(1)} %pad_clamp_fusion), kind=kCustom, calls=%fused_computation.1 | custom fusion | bytes 32896 | tf_op jit(solution)/shard_map/gather | solution.py:470
  146.6 2.3 %copy.27 = f32[8,2,128,128]{3,2,1,0:T(8,128)} copy(f32[8,2,128,128]{3,2,1,0:T(8,128)} %get-tuple-element.30) | data formatting | bytes 2097152
  (10 shorter events, 0.1 us)
Async XLA Ops:
  0.6 6.0 %copy-start = (f32[32,128,128]{2,1,0:T(8,128)S(1)}, f32[32,128,128]{2,1,0:T(8,128)}, u32[]{:S(2)}) copy-start(f32[32,128,128]{2,1,0:T(8,128)} %param.12) | copy-start | bytes 6291460
  6.6 4.6 %copy-start.1 = (f32[16]{0:T(128)S(1)}, f32[16]{0:T(128)}, u32[]{:S(2)}) copy-start(f32[16]{0:T(128)} %param.19) | copy-start | bytes 196

commit v5 on v4

--- a/solution.py
+++ b/solution.py
@@ -13,7 +13,7 @@
 f32, bf16 = jnp.float32, jnp.bfloat16
 HALF = 72
 GROUP = 8
-AHEAD = 3
+AHEAD = 5
 VMEM_BYTES = 56 * 1024 * 1024
 
 
@@ -60,15 +60,22 @@
     return halves(right), halves(left)
 
 
-def contrast_half(defocus, side):
-    pixel = jnp.arange(side, dtype=jnp.int32)
-    signed = jnp.where(pixel < side // 2, pixel, pixel - side).astype(f32)
-    rows = signed[:HALF]
-    radius = (rows[:, None] * rows[:, None] + signed[None, :] * signed[None, :]) / float(
-        (side // 2) ** 2
-    )
-    phases = defocus[:, None, None] * radius[None]
-    return -(0.995 * jnp.sin(phases) + 0.1 * jnp.cos(phases))
+def contrast_of(defocus, radius):
+    phases = defocus * radius
+    quarter = jnp.floor(phases * (2.0 / math.pi) + 0.5)
+    x = ((phases - quarter * 1.5703125) - quarter * 4.837512969970703125e-4)
+    x = x - quarter * 7.54978995489188216e-8
+    z = x * x
+    sin = x + x * z * ((-1.9515295891e-4 * z + 8.3321608736e-3) * z - 1.6666654611e-1)
+    cos = (1.0 - 0.5 * z) + z * z * (
+        (2.443315711809948e-5 * z - 1.388731625493765e-3) * z + 4.166664568298827e-2
+    )
+    turn = quarter - 4.0 * jnp.floor(quarter * 0.25)
+    odd = (turn == 1.0) | (turn == 3.0)
+    sin, cos = jnp.where(odd, cos, sin), jnp.where(odd, sin, cos)
+    sin = jnp.where(turn >= 2.0, -sin, sin)
+    cos = jnp.where((turn == 1.0) | (turn == 2.0), -cos, cos)
+    return -(0.995 * sin + 0.1 * cos)
 
 
 def shift_tables(shift_list, side):
@@ -107,8 +114,8 @@
 
 
 def gather_kernel(
-    side, owners, chunks, facts, send, references, contrast, row_table, col_table,
-    right_hi, right_lo, left_hi, left_lo, sr_hi, sr_lo, score_left, scores, total,
+    side, owners, chunks, defocus, facts, send, references, row_table, col_table,
+    right_hi, right_lo, left_hi, left_lo, sr_hi, sr_lo, score_left, scores, total, contrast,
     got, held_refs, refs, running, fact_board, info, newest, last, earlier,
     send_sem, recv_sem, fact_send, fact_recv, local_sem,
 ):
@@ -155,6 +162,17 @@
             copy(r, d).start()
 
     running[0] = jnp.zeros(running.shape[1:], f32)
+    u = lax.broadcasted_iota(jnp.int32, (HALF, side), 0)
+    v = lax.broadcasted_iota(jnp.int32, (HALF, side), 1)
+    u = jnp.where(u < side // 2, u, u - side).astype(f32)
+    v = jnp.where(v < side // 2, v, v - side).astype(f32)
+    radius = (u * u + v * v) / float((side // 2) ** 2)
+
+    def fill(d, carry):
+        contrast[d] = contrast_of(defocus[d], radius)
+        return carry
+
+    lax.fori_loop(0, contrast.shape[0], fill, 0)
     for made in local_copies:
         made.wait()
     row_pick = mirror_pick(HALF, side, side, 0)
@@ -262,22 +280,24 @@
     lax.fori_loop(0, classes, close_class, 0)
 
 
-def gather_terms(send, facts, references, tables, chunks):
+def gather_terms(send, facts, references, defocus, tables, chunks):
     owners, held, side = send.shape
     slots = held // side // chunks
     class_local = references.shape[0]
-    contrast, row_table, col_table, right, left, score_right, score_left = tables
+    row_table, col_table, right, left, score_right, score_left = tables
     lanes = score_left.shape[1]
     vmem = pl.BlockSpec(memory_space=pltpu.VMEM)
     hbm = pl.BlockSpec(memory_space=pl.ANY)
+    smem = pl.BlockSpec(memory_space=pltpu.SMEM)
     dma = pltpu.SemaphoreType.DMA
     return pl.pallas_call(
         functools.partial(gather_kernel, side, owners, chunks),
-        in_specs=[vmem, hbm, hbm] + [vmem] * 10,
-        out_specs=[vmem, vmem],
+        in_specs=[smem, vmem, hbm, hbm] + [vmem] * 9,
+        out_specs=[vmem] * 3,
         out_shape=[
             jax.ShapeDtypeStruct((chunks, owners, slots, lanes), f32),
             jax.ShapeDtypeStruct((class_local, 2 * HALF, side), f32),
+            jax.ShapeDtypeStruct((defocus.shape[0], HALF, side), f32),
         ],
         scratch_shapes=[
             pltpu.VMEM(send.shape, f32),
@@ -304,7 +324,7 @@
         ),
         name="gather_terms",
     )(
-        facts, send, references, contrast, row_table, col_table, *right, *left, *score_right, score_left
+        defocus, facts, send, references, row_table, col_table, *right, *left, *score_right, score_left
     )
 
 
@@ -327,7 +347,7 @@
 
 
 def close_kernel(
-    side, bins, groups, owners, total, found, contrast, out, home,
+    side, bins, groups, owners, owner_of, rank, total, found, contrast, out, home,
     near, mid, far, board, near_send, near_recv, far_send, far_recv, score_send, score_recv,
 ):
     mesh_ids = pl.DeviceIdType.MESH
@@ -392,10 +412,11 @@
     for made in score_copies:
         made.wait()
     board[cls] = found[cls]
-    home[...] = board[...]
-
-
-def close(total, found, contrast, groups, owners):
+    for n in range(home.shape[0]):
+        home[n : n + 1] = board[owner_of[n], pl.ds(rank[n], 1)][:, : home.shape[1]]
+
+
+def close(owner_of, rank, total, found, contrast, groups, owners, shifts):
     class_local, height, side = total.shape
     rows, per = groups // 2, class_local // groups
     pieces = math.gcd(per, 2)
@@ -403,11 +424,11 @@
     vmem = pl.BlockSpec(memory_space=pltpu.VMEM)
     return pl.pallas_call(
         functools.partial(close_kernel, side, contrast.shape[0], groups, owners),
-        in_specs=[vmem] * 3,
+        in_specs=[pl.BlockSpec(memory_space=pltpu.SMEM)] * 2 + [vmem] * 3,
         out_specs=[vmem] * 2,
         out_shape=[
             jax.ShapeDtypeStruct((per, 2, side, side), f32),
-            jax.ShapeDtypeStruct(found.shape, f32),
+            jax.ShapeDtypeStruct((owner_of.shape[0], shifts), f32),
         ],
         scratch_shapes=[
             pltpu.VMEM((rows, per, height, side), f32),
@@ -428,7 +449,7 @@
             flops=per * 20_000_000, bytes_accessed=8_000_000, transcendentals=0
         ),
         name="close",
-    )(total.reshape(rows, 2, per, height, side), found, contrast)
+    )(owner_of, rank, total.reshape(rows, 2, per, height, side), found, contrast)
 
 
 def body(
@@ -460,14 +481,15 @@
     send = particles[source].reshape(owners, capacity * side, side)
 
     right, left = dft_tables(side)
-    contrast = contrast_half(defocus, side)
     row_table, col_table, score_right, score_left = shift_tables(shift_list, side)
-    tables = (contrast, row_table, col_table, right, left, split_table(score_right), score_left)
-
-    found, total = gather_terms(send, facts, references, tables, chunks)
+    tables = (row_table, col_table, right, left, split_table(score_right), score_left)
+
+    found, total, contrast = gather_terms(send, facts, references, defocus, tables, chunks)
     found = found.transpose(1, 0, 2, 3).reshape(owners, capacity, -1)
-    fresh, home = close(total, found, contrast, lax.axis_size("grp"), owners)
-    return home.reshape(slot_total, -1)[target][:, :shifts], fresh
+    fresh, scores = close(
+        owner_of, rank, total, found, contrast, lax.axis_size("grp"), owners, shifts
+    )
+    return scores, fresh
 
 
 def solution(mesh):

time: 149 us -> 146 us (0.980)
  other arithmetic: 8.73 us -> 5.53 us
    neg x1 -> x0, other arithmetic: 3.19 us -> none  [contrast_half(): return -(0.995 * jnp.sin(phases) + 0.1 * jnp.cos(phases))]
    gather x1 -> x0, local copies, waits for them, and re-layouts: 1.92 us -> none  [body(): return (home.reshape(slot_total, -1)[target][:, :shifts], fresh)]
    unnamed x5 -> x8, local copies, waits for them, and re-layouts: 2.31 us -> 3.64 us
where the time goes in v5:
time: 146 us; the launch traced here: 145 us
  Pallas kernels  129 us (88%)
  local copies, waits for them, and re-layouts  9.91 us (7%)
  other arithmetic  5.53 us (4%)
    pallas_call x1, Pallas kernels, gather_terms(): pl.pallas_call(functools.partial(gather_kernel, side, owners, chunks), in...  101 us
    pallas_call x1, Pallas kernels, close(): pl.pallas_call(functools.partial(close_kernel, side, contrast.shape[0], g...  28 us
    unnamed x8, local copies, waits for them, and re-layouts  3.64 us

profile of v5, /device:TPU:0, one launch (start us, length us, event | category | flops | bytes accessed | tf_op | source)
XLA Modules:
  0.0 145.2 jit_solution(8937629640533149937)
XLA Ops:
  0.6 0.0 copy-start
  0.7 0.8 fusion.26
  1.5 0.0 copy-start.1
  1.5 0.2 convert_reduce_fusion.rank
  1.7 0.0 copy-start.2
  1.7 0.1 select_reduce_fusion.1
  1.8 0.8 slice_bitcast_fusion
  2.5 0.7 stack.24
  3.2 0.1 iota_compare_fusion
  3.3 0.1 select_reduce_fusion
  3.4 0.1 reshape.171
  3.5 0.6 pad.4.facts
  4.1 0.1 fusion.15
  4.2 1.0 multiply_cosine_fusion
  5.2 0.7 pad_maximum_fusion.1.col_table
  5.9 0.3 fusion.17
  6.1 0.7 fusion.1
  6.9 0.2 broadcast_multiply_fusion
  7.0 0.7 maximum_maximum_fusion.score_left
  7.8 0.6 pad_maximum_fusion.row_table
  8.4 0.0 copy-done
  8.4 2.7 %gather_fusion = f32[64,128,128]{2,1,0:T(8,128)} fusion(f32[32,128,128]{2,1,0:T(8,128)S(1)} %copy-done, s32[1024]{0:T(1024)S(1)} %pad_clamp_fusion), kind=kCustom, calls=%fused_computation | custom fusion | bytes 8388864 | tf_op jit(solution)/shard_map/gather | solution.py:481
  11.1 0.0 copy-done.1
  11.1 0.0 copy-done.2
  11.1 101.0 %gather_terms.1 = (f32[8,8,1,128]{3,2,1,0:T(1,128)}, f32[32,144,128]{2,1,0:T(8,128)}, f32[16,72,128]{2,1,0:T(8,128)}) custom-call(f32[16]{0:T(128)} %defocus.1, s32[8,8,128]{2,1,0:T(8,128)} %pad.4.facts, f32[8,1024,128]{2,1,0:T(8,128)} %bitcast.24, f32[32,2,128,128]{3,2,1,0:T(8,128)} %references.1, f32[144,64]{1,0:T(8,128)} %pad_maximum_fusion.row_table, ...), custom_call_target="tpu_custom_call" | custom-call | flops 4480000000 | bytes 30000000 | tf_op jit(solution)/shard_map/gather_terms/pallas_call | solution.py:293
  112.2 1.4 copy.24
  113.6 28.0 %close.1 = (f32[8,2,128,128]{3,2,1,0:T(8,128)}, f32[32,64]{1,0:T(8,128)}) custom-call(s32[32]{0:T(128)} %copy-done.1, s32[32]{0:T(128)} %copy-done.2, f32[2,2,8,144,128]{4,3,2,1,0:T(8,128)} %bitcast.25, f32[8,8,128]{2,1,0:T(8,128)} %bitcast.26, f32[16,72,128]{2,1,0:T(8,128)} %get-tuple-element.9.contrast), custom_call_target="tpu_custom_call" | custom-call | flops 160000000 | bytes 8000000 | tf_op jit(solution)/shard_map/close/pallas_call | solution.py:425
  141.6 1.3 copy.28
  142.9 2.3 %copy.29 = f32[8,2,128,128]{3,2,1,0:T(8,128)} copy(f32[8,2,128,128]{3,2,1,0:T(8,128)} %get-tuple-element.30) | data formatting | bytes 2097152
  (6 shorter events, 0.0 us)
Async XLA Ops:
  0.6 7.8 %copy-start = (f32[32,128,128]{2,1,0:T(8,128)S(1)}, f32[32,128,128]{2,1,0:T(8,128)}, u32[]{:S(2)}) copy-start(f32[32,128,128]{2,1,0:T(8,128)} %param.12) | copy-start | bytes 6291460
  1.5 9.7 %copy-start.1 = (s32[32]{0:T(128)}, s32[32]{0:T(128)S(1)}, u32[]{:S(2)}) copy-start(s32[32]{0:T(128)S(1)} %get-tuple-element.26.owner_of) | copy-start | bytes 388
  1.7 9.5 %copy-start.2 = (s32[32]{0:T(128)}, s32[32]{0:T(128)S(1)}, u32[]{:S(2)}) copy-start(s32[32]{0:T(128)S(1)} %convert_reduce_fusion.rank) | copy-start | bytes 388
